TPU v7x, 1024 devices: a whole 4x8x16 slice. The times are simulated.
1024 devices in a mesh: replica: 32 (over x, y_lo, core), fsdp: 32 (over y_hi, z).
Axes of the slice: x: 4, y: 8 (y_hi: 2, y_lo: 4; y = y_hi * 4 + y_lo), z: 16, core: 2. Of those that a mesh axis runs over, the one named last changes fastest.
Arguments:
- theta: bfloat16 [32, 1024, 10240], P('replica', 'fsdp'), may hold values from -6 to 6
- base: bfloat16 [1024, 10240], P('fsdp'), may hold values from -0.59765625 to 0.59765625
- momentum: float32 [1024, 10240], P(('fsdp', 'replica')), may hold values from -1.2 to 1.2
- tokens: bfloat16 [131072, 10240], P(('replica', 'fsdp')), may hold values from -6 to 6
- w_query: bfloat16 [10240, 256], P('fsdp'), may hold values from -0.0625 to 0.0625
Outputs:
- new_base: bfloat16 [1024, 10240], P('fsdp')
- new_momentum: float32 [1024, 10240], P(('fsdp', 'replica'))
- query: bfloat16 [131072, 256], P(('replica', 'fsdp'))
All inputs are finite; a program needn't handle non-finite values.
Results may differ from a plain program's by a relative error of at most 0.014.
Values may be sent and summed in bfloat16 or wider, within the bound.
No kernel may reach another device: no remote copies, remote signals or barrier semaphores. Data moves between devices by JAX's collectives and lax.ppermute only.
A program may use at most 32 MiB of HBM per device.

v0:
```python
import jax
import jax.numpy as jnp
from jax import lax
from jax.sharding import PartitionSpec as P


def on_device(theta, base, momentum, tokens, w_query):
    base_wide = base.astype(jnp.float32)
    delta = (base_wide - theta[0].astype(jnp.float32)).astype(jnp.bfloat16)
    owned = momentum.shape[0]
    total = lax.psum_scatter(delta.astype(jnp.float32), "replica", scatter_dimension=0, tiled=True)
    start_row = lax.axis_index("replica") * owned
    base_rows = lax.dynamic_slice_in_dim(base_wide, start_row, owned, 0)
    grad = total / lax.axis_size("replica")
    new_momentum = 0.9 * momentum + grad
    owner_rows = (base_rows - 0.7 * (grad + 0.9 * new_momentum)).astype(jnp.bfloat16)
    new_base = lax.all_gather(owner_rows, "replica", axis=0, tiled=True)
    gathered = lax.all_gather(w_query, "fsdp", axis=0, tiled=True)
    product = jnp.dot(tokens, gathered, preferred_element_type=jnp.float32)
    return (new_base, new_momentum, product.astype(jnp.bfloat16))


def solution(mesh):
    placed = (
        P("replica", "fsdp", None),
        P("fsdp", None),
        P(("fsdp", "replica"), None),
        P(("replica", "fsdp"), None),
        P("fsdp", None),
    )
    return jax.shard_map(
        on_device,
        mesh=mesh,
        in_specs=placed,
        out_specs=(P("fsdp", None), P(("fsdp", "replica"), None), P(("replica", "fsdp"), None)),
        check_vma=False,
    )
```

profile of v0, /device:TPU:1, one launch (start us, length us, event | category | flops | bytes accessed | tf_op | source)
XLA Modules:
  0.0 437.0 jit_solution(11064909544318841260)
XLA Ops:
  8.0 0.0 copy-start
  8.0 0.0 all-reduce.3.cloned.1.call-start
  8.1 2.6 fusion.1
  10.7 0.0 copy-start.1
  10.7 0.0 all-reduce.3.cloned.1.call-update
  10.7 0.0 copy-start.2
  10.7 0.0 all-gather.3.cloned.1.call-start
  10.8 0.5 all-gather.3.cloned.1.call-update
  11.3 0.5 copy-done.1
  11.8 1.2 convert_element_type.21
  13.0 1.3 dynamic-slice
  14.2 360.2 %all-reduce.3.cloned.1.call-done = f32[32,10240]{1,0:T(8,128)} async-done(((f32[32,10240]{1,0:T(8,128)}), f32[32,10240]{1,0:T(8,128)}) %all-reduce.3.cloned.1.call-update) | async-done | bytes 1310736
  374.5 0.0 copy-done.2
  374.5 2.5 convert_bitcast_fusion
  376.9 47.4 %all-gather = bf16[32,1,10240]{2,1,0:T(2,128)(2,1)S(1)} all-gather(bf16[1,1,10240]{2,1,0:T(2,128)(2,1)S(1)} %get-tuple-element.3), channel_id=1, replica_groups=mesh['replica'=32,'fsdp'=32] {'replica'}, dimensions={0}, use_global_device_ids=true | all-gather | bytes 675840 | tf_op jit(solution)/shard_map/all_gather | solution.py:17
  424.4 1.2 copy.10
  425.6 0.0 all-gather.3.cloned.1.call-done
  425.6 0.0 copy-done
  425.6 4.0 convolution_convert_fusion
Async XLA Ops:
  8.0 417.6 %copy-start = (bf16[128,10240]{1,0:T(8,128)(2,1)S(1)}, bf16[128,10240]{1,0:T(8,128)(2,1)}, u32[]{:S(2)}) copy-start(bf16[128,10240]{1,0:T(8,128)(2,1)} %param.8) | copy-start | bytes 7864324
  8.0 366.5 %all-reduce.3.cloned.1.call-start = ((), (), s32[]{:S(2)}) async-start(), calls=%async_computation.1 | async-start | bytes 2621440
  10.7 1.1 copy-start.1
  10.7 363.8 %copy-start.2 = (f32[1,10240]{1,0:T(1,128)S(1)}, f32[1,10240]{1,0:T(1,128)}, u32[]{:S(2)}) copy-start(f32[1,10240]{1,0:T(1,128)} %param.7) | copy-start | bytes 122884
  10.7 414.9 %all-gather.3.cloned.1.call-start = ((), (), s32[]{:S(2)}) async-start(), calls=%async_computation | async-start | bytes 5406720 | tf_op jit(solution)/shard_map/all_gather | solution.py:18
Sparse Core Ops, SparseCore 0:
  12.3 362.0 all-reduce.2
Sparse Core Ops, SparseCore 1:
  16.2 200.9 all-gather.2
where the time goes:
time: 437 us
  waiting for transfers between devices  361 us (83%)
  blocking collectives  47.4 us (11%)
  between operations  15.5 us (4%)
  other arithmetic  6.29 us (1%)
    unnamed x3, waiting for transfers between devices  361 us
    all_gather x1, blocking collectives, on_device(): new_base = lax.all_gather(owner_rows, 'replica', axis=0, tiled=True)  47.4 us
  transfers between devices with their start and end apart: 2, of which 1 were waited for; matrix products, arithmetic and copies ran while one was open for 1% of the time, Pallas kernels for 0%

commit v1 on v0

v1 whole, which is shorter than its diff:
```python
import jax
import jax.numpy as jnp
from jax import lax
from jax.experimental import pallas as pl
from jax.experimental.pallas import tpu as pltpu
from jax.sharding import Mesh, PartitionSpec as P

AXES = ("x", "yl", "c", "yh", "z")
SIZES = (4, 4, 2, 2, 16)
BF = jnp.bfloat16
F32 = jnp.float32


def weaving(core, rows):
    half = rows // 2
    to = lax.broadcasted_iota(jnp.int32, (rows, rows), 0)
    source = lax.broadcasted_iota(jnp.int32, (rows, rows), 1)
    own = jnp.where(to < half, 2 * to + core, 2 * (to - half) + 1 - core)
    return (source == own).astype(F32)


def split_kernel(where_ref, theta_ref, base_ref, keep_ref, send_ref, row_ref):
    core, row = where_ref[0], where_ref[1]
    half, rows = keep_ref.shape[0], theta_ref.shape[0]
    delta = (base_ref[...].astype(F32) - theta_ref[...].astype(F32)).astype(BF)
    apart = jnp.dot(weaving(core, rows).astype(BF), delta, preferred_element_type=F32).astype(BF)
    keep_ref[...] = apart[:half]
    send_ref[...] = apart[half:]
    chosen = (lax.broadcasted_iota(jnp.int32, (16, rows), 1) == row).astype(F32).astype(BF)
    row_ref[...] = jnp.dot(chosen, base_ref[...], preferred_element_type=F32)[:1]


def split_rows(where, theta, base, interpret=False):
    rows, width = theta.shape
    step = width // 4
    half = rows // 2
    col = lambda j, s: (0, j)
    return pl.pallas_call(
        split_kernel,
        grid_spec=pltpu.PrefetchScalarGridSpec(
            num_scalar_prefetch=1,
            grid=(width // step,),
            in_specs=[pl.BlockSpec((rows, step), col)] * 2,
            out_specs=[
                pl.BlockSpec((half, step), col),
                pl.BlockSpec((half, step), col),
                pl.BlockSpec((1, step), col),
            ],
        ),
        out_shape=[
            jax.ShapeDtypeStruct((half, width), BF),
            jax.ShapeDtypeStruct((half, width), BF),
            jax.ShapeDtypeStruct((1, width), F32),
        ],
        interpret=interpret,
    )(where, theta, base)


def weave_kernel(where_ref, mine_ref, other_ref, out_ref):
    apart = jnp.concatenate([mine_ref[...], other_ref[...]], axis=0)
    back = weaving(where_ref[0], apart.shape[0]).T.astype(BF)
    out_ref[...] = jnp.dot(back, apart, preferred_element_type=F32).astype(BF)


def weave_rows(where, mine, other, interpret=False):
    half, width = mine.shape
    step = width // 4
    col = lambda j, s: (0, j)
    return pl.pallas_call(
        weave_kernel,
        grid_spec=pltpu.PrefetchScalarGridSpec(
            num_scalar_prefetch=1,
            grid=(width // step,),
            in_specs=[pl.BlockSpec((half, step), col)] * 2,
            out_specs=pl.BlockSpec((2 * half, step), col),
        ),
        out_shape=jax.ShapeDtypeStruct((2 * half, width), BF),
        interpret=interpret,
    )(where, mine, other)


def project_kernel(nx, where_ref, tokens_ref, *refs):
    parts, swapped = refs[:nx], refs[nx : 2 * nx]
    out_ref, built, total = refs[2 * nx :]
    core, x = where_ref[0], where_ref[2]
    count, piece, cols = parts[0].shape
    step = pl.program_id(0)
    mine = pl.ds(pl.multiple_of(core * cols, cols), cols)
    other = pl.ds(pl.multiple_of((1 - core) * cols, cols), cols)
    for k in range(nx):
        at = lax.rem(x + nx - k, nx) * piece
        for shard in range(count):
            rows = pl.ds(pl.multiple_of(shard * nx * piece + at, 16), piece)
            built[rows, mine] = parts[k][shard]
            built[rows, other] = swapped[k][shard]
    part = jnp.dot(tokens_ref[...], built[...], preferred_element_type=F32)

    @pl.when(step == 0)
    def _():
        total[...] = part

    @pl.when(step > 0)
    def _():
        total[...] += part

    @pl.when(step == pl.num_programs(0) - 1)
    def _():
        out_ref[...] = total[...].astype(BF)


def project(where, tokens, parts, swapped, interpret=False):
    nx = len(parts)
    nyh, nz, piece, cols = parts[0].shape
    shards = nyh * nz
    group = min(4, nz)
    per_half = nz // group
    parts = [p.reshape(shards, piece, cols) for p in parts]
    swapped = [p.reshape(shards, piece, cols) for p in swapped]
    m, width = tokens.shape
    block = group * nx * piece

    def w_at(j, s):
        own = jnp.where(j // per_half == s[3], 0, per_half)
        return (own + lax.rem(j, per_half), 0, 0)

    w_spec = pl.BlockSpec((group, piece, cols), w_at)
    return pl.pallas_call(
        lambda *refs: project_kernel(nx, *refs),
        grid_spec=pltpu.PrefetchScalarGridSpec(
            num_scalar_prefetch=1,
            grid=(width // block,),
            in_specs=[pl.BlockSpec((m, block), lambda j, s: (0, j))] + [w_spec] * (2 * nx),
            out_specs=pl.BlockSpec((m, 2 * cols), lambda j, s: (0, 0)),
            scratch_shapes=[pltpu.VMEM((block, 2 * cols), BF), pltpu.VMEM((m, 2 * cols), F32)],
        ),
        out_shape=jax.ShapeDtypeStruct((m, 2 * cols), BF),
        compiler_params=pltpu.CompilerParams(vmem_limit_bytes=32 * 1024 * 1024),
        interpret=interpret,
    )(where, tokens, *parts, *swapped)


def after(value, *earlier):
    return lax.optimization_barrier((value,) + earlier)[0]


def on_device(sizes, interpret, theta, base, momentum, tokens, w_query):
    nx, nyl, nc, nyh, nz = sizes
    x, yl, c, yh = (lax.axis_index(name) for name in AXES[:4])
    replica = (x * nyl + yl) * nc + c
    where = jnp.stack([c, replica, x, yh]).astype(jnp.int32)
    width = base.shape[1]
    flip = [(0, 1), (1, 0)]

    keep, send, base_row = split_rows(where, theta[0], base, interpret)
    theirs = lax.ppermute(send, "c", flip)

    piece, cols = w_query.shape[0] // nx, w_query.shape[1] // nc
    mine = lax.dynamic_slice(w_query, (x * piece, c * cols), (piece, cols))
    along_z = lax.all_to_all(jnp.broadcast_to(mine, (nz, piece, cols)), "z", 0, 0, tiled=True)
    far = lax.ppermute(along_z, "yh", flip)
    pair = keep.astype(F32) + theirs.astype(F32)
    pair = after(pair.astype(BF), along_z)

    rows = lax.all_to_all(pair.reshape(nx * nyl, 1, width), ("x", "yl"), 0, 0, tiled=True)
    grad = jnp.sum(rows.astype(F32), axis=0) / (nx * nyl * nc)
    new_momentum = 0.9 * momentum + grad
    owner_row = (base_row - 0.7 * (grad + 0.9 * new_momentum)).astype(BF)

    quarter = jnp.stack([along_z, far])
    parts = [quarter] + [
        lax.ppermute(quarter, "x", [(i, (i + k) % nx) for i in range(nx)]) for k in range(1, nx)
    ]
    swapped = [lax.ppermute(p, "c", flip) for p in parts]

    spread = lax.all_to_all(jnp.broadcast_to(owner_row, (nx * nyl, 1, width)), ("x", "yl"), 0, 0, tiled=True)
    spread = spread.reshape(nx * nyl, width)
    others = lax.ppermute(spread, "c", flip)
    new_base = weave_rows(where, spread, others, interpret)

    query = project(where, tokens, parts, swapped, interpret)
    return new_base, new_momentum, query


def solution(mesh, sizes=SIZES, interpret=False):
    fine = Mesh(mesh.devices.reshape(sizes), AXES)
    replica, fsdp = AXES[:3], AXES[3:]
    placed = (
        P(replica, fsdp, None),
        P(fsdp, None),
        P(fsdp + replica, None),
        P(replica + fsdp, None),
        P(fsdp, None),
    )

    def body(*args):
        return on_device(sizes, interpret, *args)

    return jax.shard_map(
        body,
        mesh=fine,
        in_specs=placed,
        out_specs=(P(fsdp, None), P(fsdp + replica, None), P(replica + fsdp, None)),
        check_vma=False,
    )
```

time: 437 us -> 146 us (0.33)
  the two profiles are of different devices: /device:TPU:1 before, /device:TPU:75 now
where the time goes in v1:
time: 146 us; the launch traced here: 145 us
  starting transfers between devices  59.2 us (41%)
  waiting for transfers between devices  48 us (33%)
  Pallas kernels  16.8 us (12%)
  local copies, waits for them, and re-layouts  11.6 us (8%)
  other arithmetic  8.49 us (6%)
    all_to_all x1, waiting for transfers between devices, on_device(): lax.all_to_all(jnp.broadcast_to(mine, (nz, piece, cols)), 'z', 0, 0, tile...  19.2 us
    ppermute x1, waiting for transfers between devices, on_device(): far = lax.ppermute(along_z, 'yh', flip)  18.7 us
    all_to_all x1, starting transfers between devices, on_device(): lax.all_to_all(jnp.broadcast_to(mine, (nz, piece, cols)), 'z', 0, 0, tile...  17.9 us
    ppermute x4, starting transfers between devices, on_device(): swapped = [lax.ppermute(p, 'c', flip) for p in parts]  10.8 us
    ppermute x3, starting transfers between devices, on_device(): lax.ppermute(quarter, 'x', [(i, (i + k) % nx) for i in range(nx)])  9.59 us
    unnamed x15, local copies, waits for them, and re-layouts  8.45 us
    ppermute x3, waiting for transfers between devices, on_device(): lax.ppermute(quarter, 'x', [(i, (i + k) % nx) for i in range(nx)])  8.38 us
    pallas_call x1, Pallas kernels, project(): pl.pallas_call(lambda *refs: project_kernel(nx, *refs), grid_spec=pltpu.P...  8.1 us
  transfers between devices with their start and end apart: 13, of which 4 were waited for; matrix products, arithmetic and copies ran while one was open for 11% of the time, Pallas kernels for 3%

profile of v1, /device:TPU:75, one launch (start us, length us, event | category | flops | bytes accessed | tf_op | source)
XLA Modules:
  0.0 145.0 jit_solution(1364822487902268764)
XLA Ops:
  1.3 4.4 %shard_map.76 = (bf16[16,10240]{1,0:T(8,128)(2,1)}, bf16[16,10240]{1,0:T(8,128)(2,1)}, f32[1,10240]{1,0:T(1,128)}) custom-call(s32[4]{0:T(128)} %pad_add_fusion.where_ref.refs_0_, bf16[32,10240]{1,0:T(8,128)(2,1)} %bitcast.25, bf16[32,10240]{1,0:T(8,128)(2,1)} %base_ref.1), custom_call_target="tpu_custom_call" | custom-call | tf_op jit(solution)/shard_map/pallas_call | solution.py:38
  5.7 2.6 %collective-permute-start = (bf16[16,10240]{1,0:T(8,128)(2,1)}, bf16[16,10240]{1,0:T(8,128)(2,1)S(1)}, u32[]{:S(2)}, u32[]{:S(2)}) collective-permute-start(bf16[16,10240]{1,0:T(8,128)(2,1)} %get-tuple-element.9), channel_id=1, source_target_pairs={{0,32},{32,0},{1,33},{33,1},{2,34},{34,2},{3,35},{35,3},{4,36},{36... | collective-permute-start | bytes 983048 | tf_op jit(solution)/shard_map/ppermute | solution.py:155
  8.3 0.7 dynamic_slice.3
  9.0 0.8 broadcast_in_dim.6
  9.8 17.9 %all-to-all-start = ((bf16[16,80,128]{2,1,0:T(8,128)(2,1)}), bf16[16,80,128]{2,1,0:T(8,128)(2,1)S(1)}, u32[]{:S(2)}, u32[]{:S(2)}) async-start(bf16[16,80,128]{2,1,0:T(8,128)(2,1)} %broadcast_in_dim.6), calls=%async_computation | async-start | bytes 655360 | tf_op jit(solution)/shard_map/all_to_all | solution.py:159
  27.6 1.1 add_convert_fusion
  28.7 19.2 %all-to-all-done = bf16[16,80,128]{2,1,0:T(8,128)(2,1)S(1)} async-done(((bf16[16,80,128]{2,1,0:T(8,128)(2,1)}), bf16[16,80,128]{2,1,0:T(8,128)(2,1)S(1)}, u32[]{:S(2)}, u32[]{:S(2)}) %all-to-all-start) | async-done | bytes 327712 | tf_op jit(solution)/shard_map/all_to_all | solution.py:159
  48.4 0.9 reduce.3
  49.3 1.0 reshape.59
  50.2 7.2 %all-to-all-start.1 = ((bf16[16,2,5120]{2,1,0:T(2,128)(2,1)}), bf16[16,2,5120]{2,1,0:T(2,128)(2,1)S(1)}, u32[]{:S(2)}, u32[]{:S(2)}) async-start(bf16[16,2,5120]{2,1,0:T(2,128)(2,1)} %reshape.59), calls=%async_computation.1 | async-start | bytes 655360 | tf_op jit(solution)/shard_map/all_to_all | solution.py:164
  57.4 4.7 %collective-permute-start.2 = (bf16[16,80,128]{2,1,0:T(8,128)(2,1)S(1)}, bf16[16,80,128]{2,1,0:T(8,128)(2,1)S(1)}, u32[]{:S(2)}, u32[]{:S(2)}) collective-permute-start(bf16[16,80,128]{2,1,0:T(8,128)(2,1)S(1)} %all-to-all-done), channel_id=1, source_target_pairs={{0,16},{16,0},{1,17},{17,1},{2,18},{18,2},{3,19},{19,3},{4,20},{20... | collective-permute-start | bytes 983048 | tf_op jit(solution)/shard_map/ppermute | solution.py:160
  62.2 18.7 %collective-permute-done.2 = bf16[16,80,128]{2,1,0:T(8,128)(2,1)S(1)} collective-permute-done((bf16[16,80,128]{2,1,0:T(8,128)(2,1)S(1)}, bf16[16,80,128]{2,1,0:T(8,128)(2,1)S(1)}, u32[]{:S(2)}, u32[]{:S(2)}) %collective-permute-start.2) | collective-permute-done | bytes 327712 | tf_op jit(solution)/shard_map/ppermute | solution.py:160
  80.9 3.1 %collective-permute-start.3 = (bf16[2,16,80,128]{3,2,1,0:T(8,128)(2,1)S(1)}, bf16[2,16,80,128]{3,2,1,0:T(8,128)(2,1)}, u32[]{:S(2)}, u32[]{:S(2)}) collective-permute-start(bf16[2,16,80,128]{3,2,1,0:T(8,128)(2,1)S(1)} %pad_maximum_fusion), channel_id=1, source_target_pairs={{0,256},{256,512},{512,768},{768,0},{1,257},{257,513},{513,769},{7... | collective-permute-start | bytes 1966088 | tf_op jit(solution)/shard_map/ppermute | solution.py:171
  84.0 2.8 %collective-permute-start.4 = (bf16[2,16,80,128]{3,2,1,0:T(8,128)(2,1)S(1)}, bf16[2,16,80,128]{3,2,1,0:T(8,128)(2,1)}, u32[]{:S(2)}, u32[]{:S(2)}) collective-permute-start(bf16[2,16,80,128]{3,2,1,0:T(8,128)(2,1)S(1)} %pad_maximum_fusion), channel_id=1, source_target_pairs={{0,512},{256,768},{512,0},{768,256},{1,513},{257,769},{513,1},{769... | collective-permute-start | bytes 1966088 | tf_op jit(solution)/shard_map/ppermute | solution.py:171
  86.8 3.7 %collective-permute-start.5 = (bf16[2,16,80,128]{3,2,1,0:T(8,128)(2,1)S(1)}, bf16[2,16,80,128]{3,2,1,0:T(8,128)(2,1)}, u32[]{:S(2)}, u32[]{:S(2)}) collective-permute-start(bf16[2,16,80,128]{3,2,1,0:T(8,128)(2,1)S(1)} %pad_maximum_fusion), channel_id=1, source_target_pairs={{0,768},{256,0},{512,256},{768,512},{1,769},{257,1},{513,257},{769... | collective-permute-start | bytes 1966088 | tf_op jit(solution)/shard_map/ppermute | solution.py:171
  91.6 0.7 convert_reduce_fusion.1
  92.3 1.2 broadcast_in_dim.7
  93.5 4.4 %reduce.4 = bf16[16,10240]{1,0:T(8,128)(2,1)} reduce(bf16[16,1,10240]{2,1,0:T(2,128)(2,1)} %broadcast_in_dim.7, bf16[]{:T(256)} %broadcast.20), dimensions={1}, to_apply=%broadcast_in_dim.7.reduce_sub_computation | reduce | bytes 655362 | tf_op jit(solution)/shard_map/broadcast_in_dim | solution.py:175
  97.9 1.9 %reshape.61 = bf16[16,2,5120]{2,1,0:T(2,128)(2,1)} reshape(bf16[16,10240]{1,0:T(8,128)(2,1)} %reduce.4) | data formatting | bytes 655360
  99.9 4.5 %all-to-all-start.2 = ((bf16[16,2,5120]{2,1,0:T(2,128)(2,1)}), bf16[16,2,5120]{2,1,0:T(2,128)(2,1)}, u32[]{:S(2)}, u32[]{:S(2)}) async-start(bf16[16,2,5120]{2,1,0:T(2,128)(2,1)} %reshape.61), calls=%async_computation.2 | async-start | bytes 655360 | tf_op jit(solution)/shard_map/all_to_all | solution.py:175
  104.4 3.9 %collective-permute-start.6 = (bf16[2,16,80,128]{3,2,1,0:T(8,128)(2,1)S(1)}, bf16[2,16,80,128]{3,2,1,0:T(8,128)(2,1)}, u32[]{:S(2)}, u32[]{:S(2)}) collective-permute-start(bf16[2,16,80,128]{3,2,1,0:T(8,128)(2,1)S(1)} %pad_maximum_fusion), channel_id=1, source_target_pairs={{0,32},{32,0},{1,33},{33,1},{2,34},{34,2},{3,35},{35,3},{4,36},{36... | collective-permute-start | bytes 1966088 | tf_op jit(solution)/shard_map/ppermute | solution.py:173
  108.4 1.9 %collective-permute-start.7 = (bf16[2,16,80,128]{3,2,1,0:T(8,128)(2,1)}, bf16[2,16,80,128]{3,2,1,0:T(8,128)(2,1)}, u32[]{:S(2)}, u32[]{:S(2)}) collective-permute-start(bf16[2,16,80,128]{3,2,1,0:T(8,128)(2,1)} %collective-permute-done.3), channel_id=1, source_target_pairs={{0,32},{32,0},{1,33},{33,1},{2,34},{34,2},{3,35},{35,3},{4,36},{36... | collective-permute-start | bytes 1966088 | tf_op jit(solution)/shard_map/ppermute | solution.py:173
  110.3 2.4 %collective-permute-start.8 = (bf16[2,16,80,128]{3,2,1,0:T(8,128)(2,1)}, bf16[2,16,80,128]{3,2,1,0:T(8,128)(2,1)}, u32[]{:S(2)}, u32[]{:S(2)}) collective-permute-start(bf16[2,16,80,128]{3,2,1,0:T(8,128)(2,1)} %collective-permute-done.4), channel_id=1, source_target_pairs={{0,32},{32,0},{1,33},{33,1},{2,34},{34,2},{3,35},{35,3},{4,36},{36... | collective-permute-start | bytes 1966088 | tf_op jit(solution)/shard_map/ppermute | solution.py:173
  112.7 8.4 %collective-permute-done.5 = bf16[2,16,80,128]{3,2,1,0:T(8,128)(2,1)} collective-permute-done((bf16[2,16,80,128]{3,2,1,0:T(8,128)(2,1)S(1)}, bf16[2,16,80,128]{3,2,1,0:T(8,128)(2,1)}, u32[]{:S(2)}, u32[]{:S(2)}) %collective-permute-start.5) | collective-permute-done | bytes 655392 | tf_op jit(solution)/shard_map/ppermute | solution.py:171
  121.1 2.5 %collective-permute-start.9 = (bf16[2,16,80,128]{3,2,1,0:T(8,128)(2,1)}, bf16[2,16,80,128]{3,2,1,0:T(8,128)(2,1)}, u32[]{:S(2)}, u32[]{:S(2)}) collective-permute-start(bf16[2,16,80,128]{3,2,1,0:T(8,128)(2,1)} %collective-permute-done.5), channel_id=1, source_target_pairs={{0,32},{32,0},{1,33},{33,1},{2,34},{34,2},{3,35},{35,3},{4,36},{36... | collective-permute-start | bytes 1966088 | tf_op jit(solution)/shard_map/ppermute | solution.py:173
  123.6 3.2 %reshape.62 = bf16[16,1,10240]{2,1,0:T(2,128)(2,1)} reshape(bf16[16,2,5120]{2,1,0:T(2,128)(2,1)} %all-to-all-done.2) | data formatting | bytes 655360
  126.8 1.3 copy.12
  128.1 0.7 copy-done.2
  128.9 1.9 %collective-permute-start.1 = (bf16[16,10240]{1,0:T(8,128)(2,1)S(1)}, bf16[16,10240]{1,0:T(8,128)(2,1)}, u32[]{:S(2)}, u32[]{:S(2)}) collective-permute-start(bf16[16,10240]{1,0:T(8,128)(2,1)S(1)} %bitcast.23), channel_id=1, source_target_pairs={{0,32},{32,0},{1,33},{33,1},{2,34},{34,2},{3,35},{35,3},{4,36},{36... | collective-permute-start | bytes 983048 | tf_op jit(solution)/shard_map/ppermute | solution.py:177
  130.8 1.7 %collective-permute-done.1.other_ref = bf16[16,10240]{1,0:T(8,128)(2,1)} collective-permute-done((bf16[16,10240]{1,0:T(8,128)(2,1)S(1)}, bf16[16,10240]{1,0:T(8,128)(2,1)}, u32[]{:S(2)}, u32[]{:S(2)}) %collective-permute-start.1) | collective-permute-done | bytes 327712 | tf_op jit(solution)/shard_map/ppermute | solution.py:177
  132.5 4.4 %shard_map.77 = bf16[32,10240]{1,0:T(8,128)(2,1)} custom-call(s32[4]{0:T(128)} %pad_add_fusion.where_ref.refs_0_, bf16[16,10240]{1,0:T(8,128)(2,1)} %bitcast.24, bf16[16,10240]{1,0:T(8,128)(2,1)} %collective-permute-done.1.other_ref), custom_call_target="tpu_custom_call" | custom-call | tf_op jit(solution)/shard_map/pallas_call | solution.py:69
  136.9 8.1 %shard_map.78 = bf16[128,256]{1,0:T(8,128)(2,1)} custom-call(s32[4]{0:T(128)S(1)} %copy-done.1, bf16[128,10240]{1,0:T(8,128)(2,1)S(1)} %copy-done, bf16[32,80,128]{2,1,0:T(8,128)(2,1)S(1)} %bitcast.20, bf16[32,80,128]{2,1,0:T(8,128)(2,1)} %bitcast.10.refs_3_, bf16[32,80,128]{2,1,0:T(8,128)(2,1)} %bitcast.11.refs_4_, bf16[32,80,128]{2,1,0:T(8,128)(2,1)} %bitcast.12.refs_5_, ...), custom_call_target="tpu_custom_call" | custom-call | tf_op jit(solution)/shard_map/pallas_call | solution.py:127
  (24 shorter events, 2.3 us)
Async XLA Ops:
  5.7 22.0 %collective-permute-start = (bf16[16,10240]{1,0:T(8,128)(2,1)}, bf16[16,10240]{1,0:T(8,128)(2,1)S(1)}, u32[]{:S(2)}, u32[]{:S(2)}) collective-permute-start(bf16[16,10240]{1,0:T(8,128)(2,1)} %get-tuple-element.9), channel_id=1, source_target_pairs={{0,32},{32,0},{1,33},{33,1},{2,34},{34,2},{3,35},{35,3},{4,36},{36... | collective-permute-start | bytes 983048 | tf_op jit(solution)/shard_map/ppermute | solution.py:155
  9.8 38.1 %all-to-all-start = ((bf16[16,80,128]{2,1,0:T(8,128)(2,1)}), bf16[16,80,128]{2,1,0:T(8,128)(2,1)S(1)}, u32[]{:S(2)}, u32[]{:S(2)}) async-start(bf16[16,80,128]{2,1,0:T(8,128)(2,1)} %broadcast_in_dim.6), calls=%async_computation | async-start | bytes 655360 | tf_op jit(solution)/shard_map/all_to_all | solution.py:159
  28.7 62.9 %copy-start.3 = (f32[1,10240]{1,0:T(1,128)S(1)}, f32[1,10240]{1,0:T(1,128)}, u32[]{:S(2)}) copy-start(f32[1,10240]{1,0:T(1,128)} %param.7) | copy-start | bytes 122884
  28.7 62.9 %copy-start.4 = (f32[1,10240]{1,0:T(1,128)S(1)}, f32[1,10240]{1,0:T(1,128)}, u32[]{:S(2)}) copy-start(f32[1,10240]{1,0:T(1,128)} %get-tuple-element.7) | copy-start | bytes 122884
  50.2 40.3 %all-to-all-start.1 = ((bf16[16,2,5120]{2,1,0:T(2,128)(2,1)}), bf16[16,2,5120]{2,1,0:T(2,128)(2,1)S(1)}, u32[]{:S(2)}, u32[]{:S(2)}) async-start(bf16[16,2,5120]{2,1,0:T(2,128)(2,1)} %reshape.59), calls=%async_computation.1 | async-start | bytes 655360 | tf_op jit(solution)/shard_map/all_to_all | solution.py:164
  57.4 23.4 %collective-permute-start.2 = (bf16[16,80,128]{2,1,0:T(8,128)(2,1)S(1)}, bf16[16,80,128]{2,1,0:T(8,128)(2,1)S(1)}, u32[]{:S(2)}, u32[]{:S(2)}) collective-permute-start(bf16[16,80,128]{2,1,0:T(8,128)(2,1)S(1)} %all-to-all-done), channel_id=1, source_target_pairs={{0,16},{16,0},{1,17},{17,1},{2,18},{18,2},{3,19},{19,3},{4,20},{20... | collective-permute-start | bytes 983048 | tf_op jit(solution)/shard_map/ppermute | solution.py:160
  80.9 27.4 %collective-permute-start.3 = (bf16[2,16,80,128]{3,2,1,0:T(8,128)(2,1)S(1)}, bf16[2,16,80,128]{3,2,1,0:T(8,128)(2,1)}, u32[]{:S(2)}, u32[]{:S(2)}) collective-permute-start(bf16[2,16,80,128]{3,2,1,0:T(8,128)(2,1)S(1)} %pad_maximum_fusion), channel_id=1, source_target_pairs={{0,256},{256,512},{512,768},{768,0},{1,257},{257,513},{513,769},{7... | collective-permute-start | bytes 1966088 | tf_op jit(solution)/shard_map/ppermute | solution.py:171
  84.0 26.3 %collective-permute-start.4 = (bf16[2,16,80,128]{3,2,1,0:T(8,128)(2,1)S(1)}, bf16[2,16,80,128]{3,2,1,0:T(8,128)(2,1)}, u32[]{:S(2)}, u32[]{:S(2)}) collective-permute-start(bf16[2,16,80,128]{3,2,1,0:T(8,128)(2,1)S(1)} %pad_maximum_fusion), channel_id=1, source_target_pairs={{0,512},{256,768},{512,0},{768,256},{1,513},{257,769},{513,1},{769... | collective-permute-start | bytes 1966088 | tf_op jit(solution)/shard_map/ppermute | solution.py:171
  86.8 34.3 %collective-permute-start.5 = (bf16[2,16,80,128]{3,2,1,0:T(8,128)(2,1)S(1)}, bf16[2,16,80,128]{3,2,1,0:T(8,128)(2,1)}, u32[]{:S(2)}, u32[]{:S(2)}) collective-permute-start(bf16[2,16,80,128]{3,2,1,0:T(8,128)(2,1)S(1)} %pad_maximum_fusion), channel_id=1, source_target_pairs={{0,768},{256,0},{512,256},{768,512},{1,769},{257,1},{513,257},{769... | collective-permute-start | bytes 1966088 | tf_op jit(solution)/shard_map/ppermute | solution.py:171
  93.5 43.4 %copy-start = (bf16[128,10240]{1,0:T(8,128)(2,1)S(1)}, bf16[128,10240]{1,0:T(8,128)(2,1)}, u32[]{:S(2)}) copy-start(bf16[128,10240]{1,0:T(8,128)(2,1)} %refs_1_.1) | copy-start | bytes 7864324
  93.5 43.4 %copy-start.1 = (s32[4]{0:T(128)S(1)}, s32[4]{0:T(128)}, u32[]{:S(2)}) copy-start(s32[4]{0:T(128)} %pad_add_fusion.where_ref.refs_0_) | copy-start | bytes 52
  99.9 23.7 %all-to-all-start.2 = ((bf16[16,2,5120]{2,1,0:T(2,128)(2,1)}), bf16[16,2,5120]{2,1,0:T(2,128)(2,1)}, u32[]{:S(2)}, u32[]{:S(2)}) async-start(bf16[16,2,5120]{2,1,0:T(2,128)(2,1)} %reshape.61), calls=%async_computation.2 | async-start | bytes 655360 | tf_op jit(solution)/shard_map/all_to_all | solution.py:175
  104.4 32.5 %collective-permute-start.6 = (bf16[2,16,80,128]{3,2,1,0:T(8,128)(2,1)S(1)}, bf16[2,16,80,128]{3,2,1,0:T(8,128)(2,1)}, u32[]{:S(2)}, u32[]{:S(2)}) collective-permute-start(bf16[2,16,80,128]{3,2,1,0:T(8,128)(2,1)S(1)} %pad_maximum_fusion), channel_id=1, source_target_pairs={{0,32},{32,0},{1,33},{33,1},{2,34},{34,2},{3,35},{35,3},{4,36},{36... | collective-permute-start | bytes 1966088 | tf_op jit(solution)/shard_map/ppermute | solution.py:173
  108.4 28.5 %collective-permute-start.7 = (bf16[2,16,80,128]{3,2,1,0:T(8,128)(2,1)}, bf16[2,16,80,128]{3,2,1,0:T(8,128)(2,1)}, u32[]{:S(2)}, u32[]{:S(2)}) collective-permute-start(bf16[2,16,80,128]{3,2,1,0:T(8,128)(2,1)} %collective-permute-done.3), channel_id=1, source_target_pairs={{0,32},{32,0},{1,33},{33,1},{2,34},{34,2},{3,35},{35,3},{4,36},{36... | collective-permute-start | bytes 1966088 | tf_op jit(solution)/shard_map/ppermute | solution.py:173
  110.3 26.6 %collective-permute-start.8 = (bf16[2,16,80,128]{3,2,1,0:T(8,128)(2,1)}, bf16[2,16,80,128]{3,2,1,0:T(8,128)(2,1)}, u32[]{:S(2)}, u32[]{:S(2)}) collective-permute-start(bf16[2,16,80,128]{3,2,1,0:T(8,128)(2,1)} %collective-permute-done.4), channel_id=1, source_target_pairs={{0,32},{32,0},{1,33},{33,1},{2,34},{34,2},{3,35},{35,3},{4,36},{36... | collective-permute-start | bytes 1966088 | tf_op jit(solution)/shard_map/ppermute | solution.py:173
  121.1 15.8 %collective-permute-start.9 = (bf16[2,16,80,128]{3,2,1,0:T(8,128)(2,1)}, bf16[2,16,80,128]{3,2,1,0:T(8,128)(2,1)}, u32[]{:S(2)}, u32[]{:S(2)}) collective-permute-start(bf16[2,16,80,128]{3,2,1,0:T(8,128)(2,1)} %collective-permute-done.5), channel_id=1, source_target_pairs={{0,32},{32,0},{1,33},{33,1},{2,34},{34,2},{3,35},{35,3},{4,36},{36... | collective-permute-start | bytes 1966088 | tf_op jit(solution)/shard_map/ppermute | solution.py:173
  128.1 0.7 copy-start.2
  128.9 3.6 %collective-permute-start.1 = (bf16[16,10240]{1,0:T(8,128)(2,1)S(1)}, bf16[16,10240]{1,0:T(8,128)(2,1)}, u32[]{:S(2)}, u32[]{:S(2)}) collective-permute-start(bf16[16,10240]{1,0:T(8,128)(2,1)S(1)} %bitcast.23), channel_id=1, source_target_pairs={{0,32},{32,0},{1,33},{33,1},{2,34},{34,2},{3,35},{35,3},{4,36},{36... | collective-permute-start | bytes 983048 | tf_op jit(solution)/shard_map/ppermute | solution.py:177

commit v2 on v0

v2 whole, which is shorter than its diff:
```python
import jax
import jax.numpy as jnp
from jax import lax
from jax.experimental import pallas as pl
from jax.experimental.pallas import tpu as pltpu
from jax.sharding import Mesh, PartitionSpec as P

AXES = ("x", "yl", "c", "yh", "z")
SIZES = (4, 4, 2, 2, 16)
LANES = 128
BF = jnp.bfloat16
F32 = jnp.float32
COST = pl.CostEstimate(flops=0, bytes_accessed=1_000_000, transcendentals=0)
SMEM = pl.BlockSpec(memory_space=pltpu.SMEM)


def call(kernel, out_shape, scratch, interpret, *args):
    return pl.pallas_call(
        kernel,
        in_specs=[SMEM] + [pl.BlockSpec(memory_space=pltpu.VMEM)] * (len(args) - 1),
        out_shape=out_shape,
        scratch_shapes=scratch,
        compiler_params=pltpu.CompilerParams(vmem_limit_bytes=24 * 1024 * 1024),
        cost_estimate=COST,
        interpret=interpret,
    )(*args)


def split_kernel(where_ref, theta_ref, base_ref, keep_ref, send_ref, row_ref, wide, wide_base):
    core, row = where_ref[0], where_ref[1]
    rows, width = theta_ref.shape
    chunks = width // LANES
    for j in range(chunks):
        at = pl.ds(j * LANES, LANES)
        base = base_ref[:, at].astype(F32)
        wide[pl.ds(j, rows, stride=chunks), :] = base - theta_ref[:, at].astype(F32)
        wide_base[pl.ds(j, rows, stride=chunks), :] = base
    for i in range(rows // 2):
        keep_ref[i] = wide[pl.ds(pl.multiple_of((2 * i + core) * chunks, 8), chunks), :].astype(BF)
        send_ref[i] = wide[pl.ds(pl.multiple_of((2 * i + 1 - core) * chunks, 8), chunks), :].astype(BF)
    row_ref[...] = wide_base[pl.ds(pl.multiple_of(row * chunks, 8), chunks), :]


def split_rows(where, theta, base, interpret):
    rows, width = theta.shape
    chunks = width // LANES
    halves = jax.ShapeDtypeStruct((rows // 2, chunks, LANES), BF)
    return call(
        split_kernel,
        [halves, halves, jax.ShapeDtypeStruct((chunks, LANES), F32)],
        [pltpu.VMEM((rows * chunks, LANES), F32)] * 2,
        interpret,
        where,
        theta,
        base,
    )


def update_kernel(replicas, where_ref, rows_ref, momentum_ref, row_ref, momentum_out, spread_ref):
    grad = jnp.sum(rows_ref[...].astype(F32), axis=0) / replicas
    new_momentum = 0.9 * momentum_ref[...] + grad
    momentum_out[...] = new_momentum
    owner = (row_ref[...] - 0.7 * (grad + 0.9 * new_momentum)).astype(BF)
    spread_ref[...] = jnp.broadcast_to(owner[None], spread_ref.shape)


def weave_kernel(where_ref, mine_ref, other_ref, out_ref, wide):
    core = where_ref[0]
    half, chunks = mine_ref.shape[:2]
    for i in range(half):
        wide[pl.ds(pl.multiple_of((2 * i + core) * chunks, 8), chunks), :] = mine_ref[i].astype(F32)
        wide[pl.ds(pl.multiple_of((2 * i + 1 - core) * chunks, 8), chunks), :] = other_ref[i].astype(F32)
    for j in range(chunks):
        out_ref[:, pl.ds(j * LANES, LANES)] = wide[pl.ds(j, 2 * half, stride=chunks), :].astype(BF)


def deal_kernel(piece, where_ref, tokens_ref, *out_refs):
    count = len(out_refs)
    shards = out_refs[0].shape[1] // piece

    def columns(x):
        starts = [(f * count + x) * piece for f in range(shards)]
        return jnp.concatenate([tokens_ref[:, at : at + piece] for at in starts], axis=1)

    for x in range(count):

        @pl.when(where_ref[2] == x)
        def _():
            for k, out_ref in enumerate(out_refs):
                out_ref[...] = columns((x + k) % count)


def deal_tokens(where, tokens, count, piece, interpret):
    m, width = tokens.shape
    block = 8 * piece * count
    return pl.pallas_call(
        lambda *refs: deal_kernel(piece, *refs),
        grid_spec=pltpu.PrefetchScalarGridSpec(
            num_scalar_prefetch=1,
            grid=(width // block,),
            in_specs=[pl.BlockSpec((m, block), lambda j, s: (0, j))],
            out_specs=[pl.BlockSpec((m, block // count), lambda j, s: (0, j))] * count,
        ),
        out_shape=[jax.ShapeDtypeStruct((m, width // count), BF)] * count,
        cost_estimate=COST,
        interpret=interpret,
    )(where, tokens)


def project_kernel(count, where_ref, *refs):
    tokens_refs, (mine_ref, other_ref, out_ref) = refs[:count], refs[count:]
    core, x = where_ref[0], where_ref[2]
    m, cols = tokens_refs[0].shape[0], mine_ref.shape[1]
    tokens = jnp.concatenate([ref[...] for ref in tokens_refs], axis=0)
    for side, ref in ((core, mine_ref), (1 - core, other_ref)):
        part = jnp.dot(tokens, ref[...], preferred_element_type=F32).astype(BF)
        at = pl.ds(pl.multiple_of(side * cols, cols), cols)
        for k in range(count):
            out_ref[lax.rem(x + count - k, count), :, at] = part[k * m : (k + 1) * m]


def after(value, *earlier):
    return lax.optimization_barrier((value,) + earlier)[0]


def on_device(sizes, interpret, theta, base, momentum, tokens, w_query):
    nx, nyl, nc, nyh, nz = sizes
    x, yl, c, yh = (lax.axis_index(name) for name in AXES[:4])
    where = jnp.stack([c, (x * nyl + yl) * nc + c, x]).astype(jnp.int32)
    width = base.shape[1]
    chunks = width // LANES
    owners = nx * nyl
    flip = [(0, 1), (1, 0)]

    piece, cols = w_query.shape[0] // nx, w_query.shape[1] // nc
    mine = lax.dynamic_slice(w_query, (x * piece, c * cols), (piece, cols))
    mine = jnp.broadcast_to(mine, (nz, piece, cols))
    along_z = lax.all_to_all(mine, "z", 0, 0, tiled=True)

    keep, send, base_row = split_rows(where, after(theta[0], mine), base, interpret)
    theirs = lax.ppermute(send, "c", flip)

    hands = deal_tokens(where, after(tokens, send), nx, piece, interpret)
    dealt = [hands[0]] + [
        lax.ppermute(hands[k], "x", [(i, (i + k) % nx) for i in range(nx)]) for k in range(1, nx)
    ]

    along_z = after(along_z, hands[1])
    far = lax.ppermute(along_z, "yh", flip)
    pair = (after(keep, along_z).astype(F32) + theirs.astype(F32)).astype(BF)

    rows = lax.all_to_all(pair, ("x", "yl"), 0, 0, tiled=True)
    new_momentum, spread = call(
        lambda *refs: update_kernel(owners * nc, *refs),
        [jax.ShapeDtypeStruct((chunks, LANES), F32), jax.ShapeDtypeStruct((owners, chunks, LANES), BF)],
        [],
        interpret,
        where,
        rows,
        momentum.reshape(chunks, LANES),
        base_row,
    )
    dealt[0] = after(dealt[0], spread)
    spread = lax.all_to_all(spread, ("x", "yl"), 0, 0, tiled=True)

    near = jnp.where(yh == 0, along_z, far), jnp.where(yh == 0, far, along_z)
    quarter = jnp.concatenate(near).reshape(nyh * nz * piece, cols)
    swapped = lax.ppermute(quarter, "c", flip)
    product = call(
        lambda *refs: project_kernel(nx, *refs),
        jax.ShapeDtypeStruct((nx, tokens.shape[0], nc * cols), BF),
        [],
        interpret,
        where,
        *dealt,
        quarter,
        swapped,
    )
    shares = lax.all_to_all(product, "x", 0, 0, tiled=True)

    others = lax.ppermute(spread, "c", flip)
    new_base = call(
        weave_kernel,
        jax.ShapeDtypeStruct((base.shape[0], width), BF),
        [pltpu.VMEM((base.shape[0] * chunks, LANES), F32)],
        interpret,
        where,
        spread,
        others,
    )
    shares = after(shares, new_base)
    query = jnp.sum(shares.astype(F32), axis=0).astype(BF)
    return new_base, new_momentum.reshape(1, width), query


def solution(mesh, sizes=SIZES, interpret=False):
    fine = Mesh(mesh.devices.reshape(sizes), AXES)
    replica, fsdp = AXES[:3], AXES[3:]
    placed = (
        P(replica, fsdp, None),
        P(fsdp, None),
        P(fsdp + replica, None),
        P(replica + fsdp, None),
        P(fsdp, None),
    )

    def body(*args):
        return on_device(sizes, interpret, *args)

    return jax.shard_map(
        body,
        mesh=fine,
        in_specs=placed,
        out_specs=(P(fsdp, None), P(fsdp + replica, None), P(replica + fsdp, None)),
        check_vma=False,
    )
```

time: 437 us -> 112 us (0.26)
  the two profiles are of different devices: /device:TPU:1 before, /device:TPU:80 now
where the time goes in v2:
time: 112 us; the launch traced here: 111 us
  starting transfers between devices  59.1 us (53%)
  waiting for transfers between devices  29.6 us (26%)
  Pallas kernels  14 us (12%)
  local copies, waits for them, and re-layouts  3.7 us (3%)
  other arithmetic  3.38 us (3%)
    all_to_all x1, starting transfers between devices, on_device(): along_z = lax.all_to_all(mine, 'z', 0, 0, tiled=True)  18.4 us
    ppermute x3, starting transfers between devices, on_device(): lax.ppermute(hands[k], 'x', [(i, (i + k) % nx) for i in range(nx)])  11.3 us
    all_to_all x1, waiting for transfers between devices, on_device(): spread = lax.all_to_all(spread, ('x', 'yl'), 0, 0, tiled=True)  10.1 us
    all_to_all x1, waiting for transfers between devices, on_device(): along_z = lax.all_to_all(mine, 'z', 0, 0, tiled=True)  8.54 us
    pallas_call x4, Pallas kernels, call(): pl.pallas_call(kernel, in_specs=[SMEM] + [pl.BlockSpec(memory_space=pltpu...  8.49 us
    all_to_all x1, starting transfers between devices, on_device(): rows = lax.all_to_all(pair, ('x', 'yl'), 0, 0, tiled=True)  7.69 us
    all_to_all x1, starting transfers between devices, on_device(): spread = lax.all_to_all(spread, ('x', 'yl'), 0, 0, tiled=True)  6.79 us
    ppermute x1, waiting for transfers between devices, on_device(): far = lax.ppermute(along_z, 'yh', flip)  5.53 us
  transfers between devices with their start and end apart: 11, of which 4 were waited for; matrix products, arithmetic and copies ran while one was open for 2% of the time, Pallas kernels for 13%

profile of v2, /device:TPU:80, one launch (start us, length us, event | category | flops | bytes accessed | tf_op | source)
XLA Modules:
  0.0 110.6 jit_solution(10183746650824270193)
XLA Ops:
  0.6 0.7 dynamic_slice.3
  1.4 0.8 broadcast_in_dim.3
  2.1 18.4 %all-to-all-start = ((bf16[16,80,128]{2,1,0:T(8,128)(2,1)}), bf16[16,80,128]{2,1,0:T(8,128)(2,1)S(1)}, u32[]{:S(2)}, u32[]{:S(2)}) async-start(bf16[16,80,128]{2,1,0:T(8,128)(2,1)} %broadcast_in_dim.3), calls=%async_computation | async-start | bytes 655360 | tf_op jit(solution)/shard_map/all_to_all | solution.py:138
  20.6 0.1 pad_add_fusion.where_ref.refs_0_
  20.6 1.1 copy-done.1
  21.7 1.1 copy-done.2
  22.8 1.7 %shard_map.76 = (bf16[16,80,128]{2,1,0:T(8,128)(2,1)S(1)}, bf16[16,80,128]{2,1,0:T(8,128)(2,1)S(1)}, f32[80,128]{1,0:T(8,128)S(1)}) custom-call(s32[3]{0:T(128)S(1)} %pad_add_fusion.where_ref.refs_0_, bf16[32,10240]{1,0:T(8,128)(2,1)S(1)} %bitcast.9, bf16[32,10240]{1,0:T(8,128)(2,1)S(1)} %copy-done.2), custom_call_target="tpu_custom_call" | custom-call | bytes 1000000 | tf_op jit(solution)/shard_map/pallas_call | solution.py:18
  24.5 0.0 copy-start.3
  24.6 1.9 %collective-permute-start = (bf16[16,80,128]{2,1,0:T(8,128)(2,1)S(1)}, bf16[16,80,128]{2,1,0:T(8,128)(2,1)S(1)}, u32[]{:S(2)}, u32[]{:S(2)}) collective-permute-start(bf16[16,80,128]{2,1,0:T(8,128)(2,1)S(1)} %get-tuple-element.20), channel_id=1, source_target_pairs={{0,32},{32,0},{1,33},{33,1},{2,34},{34,2},{3,35},{35,3},{4,36},{36... | collective-permute-start | bytes 983048 | tf_op jit(solution)/shard_map/ppermute | solution.py:141
  26.5 5.5 %shard_map.77 = (bf16[128,2560]{1,0:T(8,128)(2,1)}, bf16[128,2560]{1,0:T(8,128)(2,1)}, bf16[128,2560]{1,0:T(8,128)(2,1)}, bf16[128,2560]{1,0:T(8,128)(2,1)}) custom-call(s32[3]{0:T(128)} %copy-done.4, bf16[128,10240]{1,0:T(8,128)(2,1)} %refs_1_), custom_call_target="tpu_custom_call" | custom-call | bytes 1000000 | tf_op jit(solution)/shard_map/pallas_call | solution.py:96
  32.0 8.5 %all-to-all-done = bf16[16,80,128]{2,1,0:T(8,128)(2,1)S(1)} async-done(((bf16[16,80,128]{2,1,0:T(8,128)(2,1)}), bf16[16,80,128]{2,1,0:T(8,128)(2,1)S(1)}, u32[]{:S(2)}, u32[]{:S(2)}) %all-to-all-start) | async-done | bytes 327712 | tf_op jit(solution)/shard_map/all_to_all | solution.py:138
  40.6 0.0 collective-permute-done
  40.6 0.8 add_convert_fusion
  41.4 7.7 %all-to-all-start.1 = ((bf16[16,80,128]{2,1,0:T(8,128)(2,1)}), bf16[16,80,128]{2,1,0:T(8,128)(2,1)S(1)}, u32[]{:S(2)}, u32[]{:S(2)}) async-start(bf16[16,80,128]{2,1,0:T(8,128)(2,1)} %add_convert_fusion), calls=%async_computation.1 | async-start | bytes 655360 | tf_op jit(solution)/shard_map/all_to_all | solution.py:152
  49.1 5.0 %collective-permute-start.5 = (bf16[16,80,128]{2,1,0:T(8,128)(2,1)S(1)}, bf16[16,80,128]{2,1,0:T(8,128)(2,1)S(1)}, u32[]{:S(2)}, u32[]{:S(2)}) collective-permute-start(bf16[16,80,128]{2,1,0:T(8,128)(2,1)S(1)} %all-to-all-done), channel_id=1, source_target_pairs={{0,16},{16,0},{1,17},{17,1},{2,18},{18,2},{3,19},{19,3},{4,20},{20... | collective-permute-start | bytes 983048 | tf_op jit(solution)/shard_map/ppermute | solution.py:149
  54.1 3.4 %collective-permute-start.2 = (bf16[128,2560]{1,0:T(8,128)(2,1)}, bf16[128,2560]{1,0:T(8,128)(2,1)S(1)}, u32[]{:S(2)}, u32[]{:S(2)}) collective-permute-start(bf16[128,2560]{1,0:T(8,128)(2,1)} %get-tuple-element.22), channel_id=1, source_target_pairs={{0,256},{256,512},{512,768},{768,0},{1,257},{257,513},{513,769},{7... | collective-permute-start | bytes 1966088 | tf_op jit(solution)/shard_map/ppermute | solution.py:145
  57.5 4.6 %collective-permute-start.3 = (bf16[128,2560]{1,0:T(8,128)(2,1)}, bf16[128,2560]{1,0:T(8,128)(2,1)S(1)}, u32[]{:S(2)}, u32[]{:S(2)}) collective-permute-start(bf16[128,2560]{1,0:T(8,128)(2,1)} %get-tuple-element.30), channel_id=1, source_target_pairs={{0,512},{256,768},{512,0},{768,256},{1,513},{257,769},{513,1},{769... | collective-permute-start | bytes 1966088 | tf_op jit(solution)/shard_map/ppermute | solution.py:145
  62.1 3.4 %collective-permute-start.4 = (bf16[128,2560]{1,0:T(8,128)(2,1)}, bf16[128,2560]{1,0:T(8,128)(2,1)}, u32[]{:S(2)}, u32[]{:S(2)}) collective-permute-start(bf16[128,2560]{1,0:T(8,128)(2,1)} %get-tuple-element.31), channel_id=1, source_target_pairs={{0,768},{256,0},{512,256},{768,512},{1,769},{257,1},{513,257},{769... | collective-permute-start | bytes 1966088 | tf_op jit(solution)/shard_map/ppermute | solution.py:145
  65.5 5.5 %collective-permute-done.5 = bf16[16,80,128]{2,1,0:T(8,128)(2,1)S(1)} collective-permute-done((bf16[16,80,128]{2,1,0:T(8,128)(2,1)S(1)}, bf16[16,80,128]{2,1,0:T(8,128)(2,1)S(1)}, u32[]{:S(2)}, u32[]{:S(2)}) %collective-permute-start.5) | collective-permute-done | bytes 327712 | tf_op jit(solution)/shard_map/ppermute | solution.py:149
  71.0 0.8 broadcast_select_fusion.1
  71.8 1.4 %shard_map.78 = (f32[80,128]{1,0:T(8,128)}, bf16[16,80,128]{2,1,0:T(8,128)(2,1)}) custom-call(s32[3]{0:T(128)S(1)} %copy-done.5, bf16[16,80,128]{2,1,0:T(8,128)(2,1)S(1)} %all-to-all-done.1.refs_1_, f32[80,128]{1,0:T(8,128)S(1)} %bitcast.10, f32[80,128]{1,0:T(8,128)S(1)} %get-tuple-element.25.refs_3_), custom_call_target="tpu_custom_call" | custom-call | bytes 1000000 | tf_op jit(solution)/shard_map/pallas_call | solution.py:18
  73.1 6.8 %all-to-all-start.2 = ((bf16[16,80,128]{2,1,0:T(8,128)(2,1)}), bf16[16,80,128]{2,1,0:T(8,128)(2,1)S(1)}, u32[]{:S(2)}, u32[]{:S(2)}) async-start(bf16[16,80,128]{2,1,0:T(8,128)(2,1)} %get-tuple-element.26), calls=%async_computation.2 | async-start | bytes 655360 | tf_op jit(solution)/shard_map/all_to_all | solution.py:164
  79.9 1.0 pad_maximum_fusion
  81.0 1.9 %collective-permute-start.6 = (bf16[2560,128]{1,0:T(8,128)(2,1)S(1)}, bf16[2560,128]{1,0:T(8,128)(2,1)}, u32[]{:S(2)}, u32[]{:S(2)}) collective-permute-start(bf16[2560,128]{1,0:T(8,128)(2,1)S(1)} %bitcast.7), channel_id=1, source_target_pairs={{0,32},{32,0},{1,33},{33,1},{2,34},{34,2},{3,35},{35,3},{4,36},{36... | collective-permute-start | bytes 1966088 | tf_op jit(solution)/shard_map/ppermute | solution.py:168
  82.9 10.1 %all-to-all-done.2.mine_ref = bf16[16,80,128]{2,1,0:T(8,128)(2,1)S(1)} async-done(((bf16[16,80,128]{2,1,0:T(8,128)(2,1)}), bf16[16,80,128]{2,1,0:T(8,128)(2,1)S(1)}, u32[]{:S(2)}, u32[]{:S(2)}) %all-to-all-start.2) | async-done | bytes 327712 | tf_op jit(solution)/shard_map/all_to_all | solution.py:164
  93.0 1.9 %collective-permute-start.1 = (bf16[16,80,128]{2,1,0:T(8,128)(2,1)S(1)}, bf16[16,80,128]{2,1,0:T(8,128)(2,1)S(1)}, u32[]{:S(2)}, u32[]{:S(2)}) collective-permute-start(bf16[16,80,128]{2,1,0:T(8,128)(2,1)S(1)} %all-to-all-done.2.mine_ref), channel_id=1, source_target_pairs={{0,32},{32,0},{1,33},{33,1},{2,34},{34,2},{3,35},{35,3},{4,36},{36... | collective-permute-start | bytes 983048 | tf_op jit(solution)/shard_map/ppermute | solution.py:181
  94.9 0.0 collective-permute-done.3.refs_3_
  95.0 3.5 %shard_map.80 = bf16[4,128,256]{2,1,0:T(8,128)(2,1)} custom-call(s32[3]{0:T(128)S(1)} %copy-done.5, bf16[128,2560]{1,0:T(8,128)(2,1)S(1)} %copy-done, bf16[128,2560]{1,0:T(8,128)(2,1)S(1)} %collective-permute-done.2.refs_2_, bf16[128,2560]{1,0:T(8,128)(2,1)S(1)} %collective-permute-done.3.refs_3_, bf16[128,2560]{1,0:T(8,128)(2,1)} %collective-permute-done.4.refs_4_, ...), custom_call_target="tpu_custom_call" | custom-call | bytes 1000000 | tf_op jit(solution)/shard_map/pallas_call | solution.py:18
  98.5 4.1 %all-to-all-start.3 = ((bf16[4,128,256]{2,1,0:T(8,128)(2,1)}), bf16[4,128,256]{2,1,0:T(8,128)(2,1)S(1)}, u32[]{:S(2)}, u32[]{:S(2)}) async-start(bf16[4,128,256]{2,1,0:T(8,128)(2,1)} %shard_map.80), calls=%async_computation.3 | async-start | bytes 524288 | tf_op jit(solution)/shard_map/all_to_all | solution.py:179
  102.6 1.9 %shard_map.79 = bf16[32,10240]{1,0:T(8,128)(2,1)} custom-call(s32[3]{0:T(128)S(1)} %copy-done.5, bf16[16,80,128]{2,1,0:T(8,128)(2,1)S(1)} %all-to-all-done.2.mine_ref, bf16[16,80,128]{2,1,0:T(8,128)(2,1)S(1)} %collective-permute-done.1.other_ref), custom_call_target="tpu_custom_call" | custom-call | bytes 1000000 | tf_op jit(solution)/shard_map/pallas_call | solution.py:18
  104.5 5.4 %all-to-all-done.3 = bf16[4,128,256]{2,1,0:T(8,128)(2,1)S(1)} async-done(((bf16[4,128,256]{2,1,0:T(8,128)(2,1)}), bf16[4,128,256]{2,1,0:T(8,128)(2,1)S(1)}, u32[]{:S(2)}, u32[]{:S(2)}) %all-to-all-start.3) | async-done | bytes 262176 | tf_op jit(solution)/shard_map/all_to_all | solution.py:179
  109.9 0.7 reduce_sum.12
  (14 shorter events, 0.0 us)
Async XLA Ops:
  2.1 38.4 %all-to-all-start = ((bf16[16,80,128]{2,1,0:T(8,128)(2,1)}), bf16[16,80,128]{2,1,0:T(8,128)(2,1)S(1)}, u32[]{:S(2)}, u32[]{:S(2)}) async-start(bf16[16,80,128]{2,1,0:T(8,128)(2,1)} %broadcast_in_dim.3), calls=%async_computation | async-start | bytes 655360 | tf_op jit(solution)/shard_map/all_to_all | solution.py:138
  20.6 1.1 copy-start.1
  21.7 1.1 copy-start.2
  22.8 3.7 %copy-start.4 = (s32[3]{0:T(128)}, s32[3]{0:T(128)S(1)}, u32[]{:S(2)}) copy-start(s32[3]{0:T(128)S(1)} %pad_add_fusion.where_ref.refs_0_) | copy-start | bytes 40
  24.5 47.2 %copy-start.3 = (f32[1,10240]{1,0:T(1,128)S(1)}, f32[1,10240]{1,0:T(1,128)}, u32[]{:S(2)}) copy-start(f32[1,10240]{1,0:T(1,128)} %param.7) | copy-start | bytes 122884
  24.6 16.0 %collective-permute-start = (bf16[16,80,128]{2,1,0:T(8,128)(2,1)S(1)}, bf16[16,80,128]{2,1,0:T(8,128)(2,1)S(1)}, u32[]{:S(2)}, u32[]{:S(2)}) collective-permute-start(bf16[16,80,128]{2,1,0:T(8,128)(2,1)S(1)} %get-tuple-element.20), channel_id=1, source_target_pairs={{0,32},{32,0},{1,33},{33,1},{2,34},{34,2},{3,35},{35,3},{4,36},{36... | collective-permute-start | bytes 983048 | tf_op jit(solution)/shard_map/ppermute | solution.py:141
  32.0 39.8 %copy-start.5 = (s32[3]{0:T(128)S(1)}, s32[3]{0:T(128)}, u32[]{:S(2)}) copy-start(s32[3]{0:T(128)} %copy-done.4) | copy-start | bytes 40
  40.6 54.4 %copy-start = (bf16[128,2560]{1,0:T(8,128)(2,1)S(1)}, bf16[128,2560]{1,0:T(8,128)(2,1)}, u32[]{:S(2)}) copy-start(bf16[128,2560]{1,0:T(8,128)(2,1)} %get-tuple-element.29.refs_1_) | copy-start | bytes 1966084
  41.4 30.4 %all-to-all-start.1 = ((bf16[16,80,128]{2,1,0:T(8,128)(2,1)}), bf16[16,80,128]{2,1,0:T(8,128)(2,1)S(1)}, u32[]{:S(2)}, u32[]{:S(2)}) async-start(bf16[16,80,128]{2,1,0:T(8,128)(2,1)} %add_convert_fusion), calls=%async_computation.1 | async-start | bytes 655360 | tf_op jit(solution)/shard_map/all_to_all | solution.py:152
  49.1 21.9 %collective-permute-start.5 = (bf16[16,80,128]{2,1,0:T(8,128)(2,1)S(1)}, bf16[16,80,128]{2,1,0:T(8,128)(2,1)S(1)}, u32[]{:S(2)}, u32[]{:S(2)}) collective-permute-start(bf16[16,80,128]{2,1,0:T(8,128)(2,1)S(1)} %all-to-all-done), channel_id=1, source_target_pairs={{0,16},{16,0},{1,17},{17,1},{2,18},{18,2},{3,19},{19,3},{4,20},{20... | collective-permute-start | bytes 983048 | tf_op jit(solution)/shard_map/ppermute | solution.py:149
  54.1 40.8 %collective-permute-start.2 = (bf16[128,2560]{1,0:T(8,128)(2,1)}, bf16[128,2560]{1,0:T(8,128)(2,1)S(1)}, u32[]{:S(2)}, u32[]{:S(2)}) collective-permute-start(bf16[128,2560]{1,0:T(8,128)(2,1)} %get-tuple-element.22), channel_id=1, source_target_pairs={{0,256},{256,512},{512,768},{768,0},{1,257},{257,513},{513,769},{7... | collective-permute-start | bytes 1966088 | tf_op jit(solution)/shard_map/ppermute | solution.py:145
  57.5 37.4 %collective-permute-start.3 = (bf16[128,2560]{1,0:T(8,128)(2,1)}, bf16[128,2560]{1,0:T(8,128)(2,1)S(1)}, u32[]{:S(2)}, u32[]{:S(2)}) collective-permute-start(bf16[128,2560]{1,0:T(8,128)(2,1)} %get-tuple-element.30), channel_id=1, source_target_pairs={{0,512},{256,768},{512,0},{768,256},{1,513},{257,769},{513,1},{769... | collective-permute-start | bytes 1966088 | tf_op jit(solution)/shard_map/ppermute | solution.py:145
  62.1 32.8 %collective-permute-start.4 = (bf16[128,2560]{1,0:T(8,128)(2,1)}, bf16[128,2560]{1,0:T(8,128)(2,1)}, u32[]{:S(2)}, u32[]{:S(2)}) collective-permute-start(bf16[128,2560]{1,0:T(8,128)(2,1)} %get-tuple-element.31), channel_id=1, source_target_pairs={{0,768},{256,0},{512,256},{768,512},{1,769},{257,1},{513,257},{769... | collective-permute-start | bytes 1966088 | tf_op jit(solution)/shard_map/ppermute | solution.py:145
  73.1 19.8 %all-to-all-start.2 = ((bf16[16,80,128]{2,1,0:T(8,128)(2,1)}), bf16[16,80,128]{2,1,0:T(8,128)(2,1)S(1)}, u32[]{:S(2)}, u32[]{:S(2)}) async-start(bf16[16,80,128]{2,1,0:T(8,128)(2,1)} %get-tuple-element.26), calls=%async_computation.2 | async-start | bytes 655360 | tf_op jit(solution)/shard_map/all_to_all | solution.py:164
  81.0 14.0 %collective-permute-start.6 = (bf16[2560,128]{1,0:T(8,128)(2,1)S(1)}, bf16[2560,128]{1,0:T(8,128)(2,1)}, u32[]{:S(2)}, u32[]{:S(2)}) collective-permute-start(bf16[2560,128]{1,0:T(8,128)(2,1)S(1)} %bitcast.7), channel_id=1, source_target_pairs={{0,32},{32,0},{1,33},{33,1},{2,34},{34,2},{3,35},{35,3},{4,36},{36... | collective-permute-start | bytes 1966088 | tf_op jit(solution)/shard_map/ppermute | solution.py:168
  93.0 9.6 %collective-permute-start.1 = (bf16[16,80,128]{2,1,0:T(8,128)(2,1)S(1)}, bf16[16,80,128]{2,1,0:T(8,128)(2,1)S(1)}, u32[]{:S(2)}, u32[]{:S(2)}) collective-permute-start(bf16[16,80,128]{2,1,0:T(8,128)(2,1)S(1)} %all-to-all-done.2.mine_ref), channel_id=1, source_target_pairs={{0,32},{32,0},{1,33},{33,1},{2,34},{34,2},{3,35},{35,3},{4,36},{36... | collective-permute-start | bytes 983048 | tf_op jit(solution)/shard_map/ppermute | solution.py:181
  98.5 11.5 %all-to-all-start.3 = ((bf16[4,128,256]{2,1,0:T(8,128)(2,1)}), bf16[4,128,256]{2,1,0:T(8,128)(2,1)S(1)}, u32[]{:S(2)}, u32[]{:S(2)}) async-start(bf16[4,128,256]{2,1,0:T(8,128)(2,1)} %shard_map.80), calls=%async_computation.3 | async-start | bytes 524288 | tf_op jit(solution)/shard_map/all_to_all | solution.py:179

commit v3 on v2

--- a/solution.py
+++ b/solution.py
@@ -90,15 +90,20 @@
                 out_ref[...] = columns((x + k) % count)
 
 
-def deal_tokens(where, tokens, count, piece, interpret):
+def deal_tokens(where, tokens, count, piece, halves, group, interpret):
     m, width = tokens.shape
-    block = 8 * piece * count
+    block = group * piece * count
+    blocks = width // block
+
+    def own_first(j, s):
+        return 0, lax.rem(j + s[3] * (blocks // halves), blocks)
+
     return pl.pallas_call(
         lambda *refs: deal_kernel(piece, *refs),
         grid_spec=pltpu.PrefetchScalarGridSpec(
             num_scalar_prefetch=1,
-            grid=(width // block,),
-            in_specs=[pl.BlockSpec((m, block), lambda j, s: (0, j))],
+            grid=(blocks,),
+            in_specs=[pl.BlockSpec((m, block), own_first)],
             out_specs=[pl.BlockSpec((m, block // count), lambda j, s: (0, j))] * count,
         ),
         out_shape=[jax.ShapeDtypeStruct((m, width // count), BF)] * count,
@@ -108,15 +113,14 @@
 
 
 def project_kernel(count, where_ref, *refs):
-    tokens_refs, (mine_ref, other_ref, out_ref) = refs[:count], refs[count:]
+    tokens_refs, (mine_ref, other_ref, out_ref, built) = refs[:count], refs[count:]
     core, x = where_ref[0], where_ref[2]
-    m, cols = tokens_refs[0].shape[0], mine_ref.shape[1]
-    tokens = jnp.concatenate([ref[...] for ref in tokens_refs], axis=0)
+    cols = mine_ref.shape[1]
     for side, ref in ((core, mine_ref), (1 - core, other_ref)):
-        part = jnp.dot(tokens, ref[...], preferred_element_type=F32).astype(BF)
-        at = pl.ds(pl.multiple_of(side * cols, cols), cols)
-        for k in range(count):
-            out_ref[lax.rem(x + count - k, count), :, at] = part[k * m : (k + 1) * m]
+        built[:, pl.ds(pl.multiple_of(side * cols, cols), cols)] = ref[...]
+    for k, ref in enumerate(tokens_refs):
+        part = jnp.dot(ref[...], built[...], preferred_element_type=F32)
+        out_ref[lax.rem(x + count - k, count)] = part.astype(BF)
 
 
 def after(value, *earlier):
@@ -126,7 +130,7 @@
 def on_device(sizes, interpret, theta, base, momentum, tokens, w_query):
     nx, nyl, nc, nyh, nz = sizes
     x, yl, c, yh = (lax.axis_index(name) for name in AXES[:4])
-    where = jnp.stack([c, (x * nyl + yl) * nc + c, x]).astype(jnp.int32)
+    where = jnp.stack([c, (x * nyl + yl) * nc + c, x, yh]).astype(jnp.int32)
     width = base.shape[1]
     chunks = width // LANES
     owners = nx * nyl
@@ -140,13 +144,14 @@
     keep, send, base_row = split_rows(where, after(theta[0], mine), base, interpret)
     theirs = lax.ppermute(send, "c", flip)
 
-    hands = deal_tokens(where, after(tokens, send), nx, piece, interpret)
+    hands = deal_tokens(where, after(tokens, send), nx, piece, nyh, nz // 2, interpret)
     dealt = [hands[0]] + [
         lax.ppermute(hands[k], "x", [(i, (i + k) % nx) for i in range(nx)]) for k in range(1, nx)
     ]
 
     along_z = after(along_z, hands[1])
     far = lax.ppermute(along_z, "yh", flip)
+    far = after(far, dealt[2])
     pair = (after(keep, along_z).astype(F32) + theirs.astype(F32)).astype(BF)
 
     rows = lax.all_to_all(pair, ("x", "yl"), 0, 0, tiled=True)
@@ -163,13 +168,12 @@
     dealt[0] = after(dealt[0], spread)
     spread = lax.all_to_all(spread, ("x", "yl"), 0, 0, tiled=True)
 
-    near = jnp.where(yh == 0, along_z, far), jnp.where(yh == 0, far, along_z)
-    quarter = jnp.concatenate(near).reshape(nyh * nz * piece, cols)
+    quarter = jnp.concatenate([along_z, far]).reshape(nyh * nz * piece, cols)
     swapped = lax.ppermute(quarter, "c", flip)
     product = call(
         lambda *refs: project_kernel(nx, *refs),
         jax.ShapeDtypeStruct((nx, tokens.shape[0], nc * cols), BF),
-        [],
+        [pltpu.VMEM((quarter.shape[0], nc * cols), BF)],
         interpret,
         where,
         *dealt,
@@ -178,7 +182,7 @@
     )
     shares = lax.all_to_all(product, "x", 0, 0, tiled=True)
 
-    others = lax.ppermute(spread, "c", flip)
+    others = lax.ppermute(after(spread, product), "c", flip)
     new_base = call(
         weave_kernel,
         jax.ShapeDtypeStruct((base.shape[0], width), BF),

time: 112 us -> 108 us (0.964)
  the two profiles are of different devices: /device:TPU:80 before, /device:TPU:1 now
where the time goes in v3:
time: 108 us; the launch traced here: 107 us
  starting transfers between devices  72.9 us (68%)
  waiting for transfers between devices  14.2 us (13%)
  Pallas kernels  13.7 us (13%)
  local copies, waits for them, and re-layouts  3.69 us (3%)
  other arithmetic  1.63 us (2%)
    all_to_all x1, starting transfers between devices, on_device(): along_z = lax.all_to_all(mine, 'z', 0, 0, tiled=True)  19.4 us
    all_to_all x1, starting transfers between devices, on_device(): spread = lax.all_to_all(spread, ('x', 'yl'), 0, 0, tiled=True)  12.5 us
    ppermute x3, starting transfers between devices, on_device(): lax.ppermute(hands[k], 'x', [(i, (i + k) % nx) for i in range(nx)])  11.2 us
    ppermute x1, starting transfers between devices, on_device(): swapped = lax.ppermute(quarter, 'c', flip)  9.11 us
    all_to_all x1, waiting for transfers between devices, on_device(): spread = lax.all_to_all(spread, ('x', 'yl'), 0, 0, tiled=True)  8.63 us
    pallas_call x4, Pallas kernels, call(): pl.pallas_call(kernel, in_specs=[SMEM] + [pl.BlockSpec(memory_space=pltpu...  8.12 us
    ppermute x1, starting transfers between devices, on_device(): far = lax.ppermute(along_z, 'yh', flip)  5.7 us
    pallas_call x1, Pallas kernels, deal_tokens(): pl.pallas_call(lambda *refs: deal_kernel(piece, *refs), grid_spec=pltpu.P...  5.57 us
  transfers between devices with their start and end apart: 11, of which 3 were waited for; matrix products, arithmetic and copies ran while one was open for 1% of the time, Pallas kernels for 13%

profile of v3, /device:TPU:1, one launch (start us, length us, event | category | flops | bytes accessed | tf_op | source)
XLA Modules:
  0.0 106.9 jit_solution(13914577680673265140)
XLA Ops:
  0.6 0.7 dynamic_slice.3
  1.4 0.8 broadcast_in_dim.3
  2.1 19.4 %all-to-all-start = ((bf16[16,80,128]{2,1,0:T(8,128)(2,1)}), bf16[16,80,128]{2,1,0:T(8,128)(2,1)S(1)}, u32[]{:S(2)}, u32[]{:S(2)}) async-start(bf16[16,80,128]{2,1,0:T(8,128)(2,1)} %broadcast_in_dim.3), calls=%async_computation | async-start | bytes 655360 | tf_op jit(solution)/shard_map/all_to_all | solution.py:142
  21.6 0.1 pad_add_fusion.where_ref.refs_0_
  21.6 1.1 %copy-done.1 = bf16[1,32,10240]{2,1,0:T(8,128)(2,1)S(1)} copy-done((bf16[1,32,10240]{2,1,0:T(8,128)(2,1)S(1)}, bf16[1,32,10240]{2,1,0:T(8,128)(2,1)}, u32[]{:S(2)}) %copy-start.1) | copy-done | bytes 655384
  22.7 1.1 %copy-done.2 = bf16[32,10240]{1,0:T(8,128)(2,1)S(1)} copy-done((bf16[32,10240]{1,0:T(8,128)(2,1)S(1)}, bf16[32,10240]{1,0:T(8,128)(2,1)}, u32[]{:S(2)}) %copy-start.2) | copy-done | bytes 655384
  23.8 1.7 %shard_map.76 = (bf16[16,80,128]{2,1,0:T(8,128)(2,1)S(1)}, bf16[16,80,128]{2,1,0:T(8,128)(2,1)S(1)}, f32[80,128]{1,0:T(8,128)S(1)}) custom-call(s32[4]{0:T(128)S(1)} %pad_add_fusion.where_ref.refs_0_, bf16[32,10240]{1,0:T(8,128)(2,1)S(1)} %bitcast.10, bf16[32,10240]{1,0:T(8,128)(2,1)S(1)} %copy-done.2), custom_call_target="tpu_custom_call" | custom-call | bytes 1000000 | tf_op jit(solution)/shard_map/pallas_call | solution.py:18
  25.5 0.0 copy-start.3
  25.6 2.9 %collective-permute-start = (bf16[16,80,128]{2,1,0:T(8,128)(2,1)S(1)}, bf16[16,80,128]{2,1,0:T(8,128)(2,1)S(1)}, u32[]{:S(2)}, u32[]{:S(2)}) collective-permute-start(bf16[16,80,128]{2,1,0:T(8,128)(2,1)S(1)} %get-tuple-element.22), channel_id=1, source_target_pairs={{0,32},{32,0},{1,33},{33,1},{2,34},{34,2},{3,35},{35,3},{4,36},{36... | collective-permute-start | bytes 983048 | tf_op jit(solution)/shard_map/ppermute | solution.py:145
  28.4 5.6 %shard_map.77 = (bf16[128,2560]{1,0:T(8,128)(2,1)}, bf16[128,2560]{1,0:T(8,128)(2,1)}, bf16[128,2560]{1,0:T(8,128)(2,1)}, bf16[128,2560]{1,0:T(8,128)(2,1)}) custom-call(s32[4]{0:T(128)} %copy-done.4, bf16[128,10240]{1,0:T(8,128)(2,1)} %refs_1_), custom_call_target="tpu_custom_call" | custom-call | bytes 1000000 | tf_op jit(solution)/shard_map/pallas_call | solution.py:101
  34.0 4.7 %collective-permute-start.2 = (bf16[128,2560]{1,0:T(8,128)(2,1)}, bf16[128,2560]{1,0:T(8,128)(2,1)S(1)}, u32[]{:S(2)}, u32[]{:S(2)}) collective-permute-start(bf16[128,2560]{1,0:T(8,128)(2,1)} %get-tuple-element.31), channel_id=1, source_target_pairs={{0,512},{256,768},{512,0},{768,256},{1,513},{257,769},{513,1},{769... | collective-permute-start | bytes 1966088 | tf_op jit(solution)/shard_map/ppermute | solution.py:149
  38.8 0.0 all-to-all-done
  38.8 0.0 collective-permute-done
  38.8 0.8 add_convert_fusion
  39.6 5.3 %all-to-all-start.1 = ((bf16[16,80,128]{2,1,0:T(8,128)(2,1)}), bf16[16,80,128]{2,1,0:T(8,128)(2,1)S(1)}, u32[]{:S(2)}, u32[]{:S(2)}) async-start(bf16[16,80,128]{2,1,0:T(8,128)(2,1)} %add_convert_fusion), calls=%async_computation.1 | async-start | bytes 655360 | tf_op jit(solution)/shard_map/all_to_all | solution.py:157
  44.9 5.7 %collective-permute-start.4 = (bf16[16,80,128]{2,1,0:T(8,128)(2,1)S(1)}, bf16[16,80,128]{2,1,0:T(8,128)(2,1)S(1)}, u32[]{:S(2)}, u32[]{:S(2)}) collective-permute-start(bf16[16,80,128]{2,1,0:T(8,128)(2,1)S(1)} %all-to-all-done), channel_id=1, source_target_pairs={{0,16},{16,0},{1,17},{17,1},{2,18},{18,2},{3,19},{19,3},{4,20},{20... | collective-permute-start | bytes 983048 | tf_op jit(solution)/shard_map/ppermute | solution.py:153
  50.6 3.2 %collective-permute-start.1 = (bf16[128,2560]{1,0:T(8,128)(2,1)}, bf16[128,2560]{1,0:T(8,128)(2,1)S(1)}, u32[]{:S(2)}, u32[]{:S(2)}) collective-permute-start(bf16[128,2560]{1,0:T(8,128)(2,1)} %get-tuple-element.24), channel_id=1, source_target_pairs={{0,256},{256,512},{512,768},{768,0},{1,257},{257,513},{513,769},{7... | collective-permute-start | bytes 1966088 | tf_op jit(solution)/shard_map/ppermute | solution.py:149
  53.8 3.3 %collective-permute-start.3 = (bf16[128,2560]{1,0:T(8,128)(2,1)}, bf16[128,2560]{1,0:T(8,128)(2,1)}, u32[]{:S(2)}, u32[]{:S(2)}) collective-permute-start(bf16[128,2560]{1,0:T(8,128)(2,1)} %get-tuple-element.32), channel_id=1, source_target_pairs={{0,768},{256,0},{512,256},{768,512},{1,769},{257,1},{513,257},{769... | collective-permute-start | bytes 1966088 | tf_op jit(solution)/shard_map/ppermute | solution.py:149
  57.1 0.0 collective-permute-done.2.refs_3_
  57.1 0.7 collective-permute-done.4
  57.8 0.1 pad_maximum_fusion
  57.9 9.1 %collective-permute-start.5 = (bf16[2560,128]{1,0:T(8,128)(2,1)S(1)}, bf16[2560,128]{1,0:T(8,128)(2,1)}, u32[]{:S(2)}, u32[]{:S(2)}) collective-permute-start(bf16[2560,128]{1,0:T(8,128)(2,1)S(1)} %bitcast.8), channel_id=1, source_target_pairs={{0,32},{32,0},{1,33},{33,1},{2,34},{34,2},{3,35},{35,3},{4,36},{36... | collective-permute-start | bytes 1966088 | tf_op jit(solution)/shard_map/ppermute | solution.py:172
  67.0 0.0 all-to-all-done.1.refs_1_
  67.0 1.4 %shard_map.78 = (f32[80,128]{1,0:T(8,128)}, bf16[16,80,128]{2,1,0:T(8,128)(2,1)}) custom-call(s32[4]{0:T(128)S(1)} %copy-done.5, bf16[16,80,128]{2,1,0:T(8,128)(2,1)S(1)} %all-to-all-done.1.refs_1_, f32[80,128]{1,0:T(8,128)S(1)} %bitcast.11, f32[80,128]{1,0:T(8,128)S(1)} %get-tuple-element.27.refs_3_), custom_call_target="tpu_custom_call" | custom-call | bytes 1000000 | tf_op jit(solution)/shard_map/pallas_call | solution.py:18
  68.4 12.5 %all-to-all-start.2 = ((bf16[16,80,128]{2,1,0:T(8,128)(2,1)}), bf16[16,80,128]{2,1,0:T(8,128)(2,1)S(1)}, u32[]{:S(2)}, u32[]{:S(2)}) async-start(bf16[16,80,128]{2,1,0:T(8,128)(2,1)} %get-tuple-element.28), calls=%async_computation.2 | async-start | bytes 655360 | tf_op jit(solution)/shard_map/all_to_all | solution.py:169
  81.0 3.2 %shard_map.79 = bf16[4,128,256]{2,1,0:T(8,128)(2,1)} custom-call(s32[4]{0:T(128)S(1)} %copy-done.5, bf16[128,2560]{1,0:T(8,128)(2,1)S(1)} %copy-done, bf16[128,2560]{1,0:T(8,128)(2,1)S(1)} %collective-permute-done.1.refs_2_, bf16[128,2560]{1,0:T(8,128)(2,1)S(1)} %collective-permute-done.2.refs_3_, bf16[128,2560]{1,0:T(8,128)(2,1)} %collective-permute-done.3.refs_4_, ...), custom_call_target="tpu_custom_call" | custom-call | bytes 1000000 | tf_op jit(solution)/shard_map/pallas_call | solution.py:18
  84.1 8.6 %all-to-all-done.2.mine_ref = bf16[16,80,128]{2,1,0:T(8,128)(2,1)S(1)} async-done(((bf16[16,80,128]{2,1,0:T(8,128)(2,1)}), bf16[16,80,128]{2,1,0:T(8,128)(2,1)S(1)}, u32[]{:S(2)}, u32[]{:S(2)}) %all-to-all-start.2) | async-done | bytes 327712 | tf_op jit(solution)/shard_map/all_to_all | solution.py:169
  92.7 3.3 %collective-permute-start.6 = (bf16[16,80,128]{2,1,0:T(8,128)(2,1)S(1)}, bf16[16,80,128]{2,1,0:T(8,128)(2,1)S(1)}, u32[]{:S(2)}, u32[]{:S(2)}) collective-permute-start(bf16[16,80,128]{2,1,0:T(8,128)(2,1)S(1)} %all-to-all-done.2.mine_ref), channel_id=1, source_target_pairs={{0,32},{32,0},{1,33},{33,1},{2,34},{34,2},{3,35},{35,3},{4,36},{36... | collective-permute-start | bytes 983048 | tf_op jit(solution)/shard_map/ppermute | solution.py:185
  96.1 3.4 %all-to-all-start.3 = ((bf16[4,128,256]{2,1,0:T(8,128)(2,1)}), bf16[4,128,256]{2,1,0:T(8,128)(2,1)S(1)}, u32[]{:S(2)}, u32[]{:S(2)}) async-start(bf16[4,128,256]{2,1,0:T(8,128)(2,1)} %shard_map.79), calls=%async_computation.3 | async-start | bytes 524288 | tf_op jit(solution)/shard_map/all_to_all | solution.py:183
  99.5 1.9 %shard_map.80 = bf16[32,10240]{1,0:T(8,128)(2,1)} custom-call(s32[4]{0:T(128)S(1)} %copy-done.5, bf16[16,80,128]{2,1,0:T(8,128)(2,1)S(1)} %all-to-all-done.2.mine_ref, bf16[16,80,128]{2,1,0:T(8,128)(2,1)S(1)} %collective-permute-done.6.other_ref), custom_call_target="tpu_custom_call" | custom-call | bytes 1000000 | tf_op jit(solution)/shard_map/pallas_call | solution.py:18
  101.4 4.9 %all-to-all-done.3 = bf16[4,128,256]{2,1,0:T(8,128)(2,1)S(1)} async-done(((bf16[4,128,256]{2,1,0:T(8,128)(2,1)}), bf16[4,128,256]{2,1,0:T(8,128)(2,1)S(1)}, u32[]{:S(2)}, u32[]{:S(2)}) %all-to-all-start.3) | async-done | bytes 262176 | tf_op jit(solution)/shard_map/all_to_all | solution.py:183
  106.3 0.7 reduce_sum.12
  (13 shorter events, 0.0 us)
Async XLA Ops:
  2.1 36.6 %all-to-all-start = ((bf16[16,80,128]{2,1,0:T(8,128)(2,1)}), bf16[16,80,128]{2,1,0:T(8,128)(2,1)S(1)}, u32[]{:S(2)}, u32[]{:S(2)}) async-start(bf16[16,80,128]{2,1,0:T(8,128)(2,1)} %broadcast_in_dim.3), calls=%async_computation | async-start | bytes 655360 | tf_op jit(solution)/shard_map/all_to_all | solution.py:142
  21.6 1.1 %copy-start.1 = (bf16[1,32,10240]{2,1,0:T(8,128)(2,1)S(1)}, bf16[1,32,10240]{2,1,0:T(8,128)(2,1)}, u32[]{:S(2)}) copy-start(bf16[1,32,10240]{2,1,0:T(8,128)(2,1)} %param.5) | copy-start | bytes 1966084
  22.7 1.1 %copy-start.2 = (bf16[32,10240]{1,0:T(8,128)(2,1)S(1)}, bf16[32,10240]{1,0:T(8,128)(2,1)}, u32[]{:S(2)}) copy-start(bf16[32,10240]{1,0:T(8,128)(2,1)} %base_ref.1) | copy-start | bytes 1966084
  23.8 4.6 %copy-start.4 = (s32[4]{0:T(128)}, s32[4]{0:T(128)S(1)}, u32[]{:S(2)}) copy-start(s32[4]{0:T(128)S(1)} %pad_add_fusion.where_ref.refs_0_) | copy-start | bytes 52
  25.5 41.5 %copy-start.3 = (f32[1,10240]{1,0:T(1,128)S(1)}, f32[1,10240]{1,0:T(1,128)}, u32[]{:S(2)}) copy-start(f32[1,10240]{1,0:T(1,128)} %param.7) | copy-start | bytes 122884
  25.6 13.2 %collective-permute-start = (bf16[16,80,128]{2,1,0:T(8,128)(2,1)S(1)}, bf16[16,80,128]{2,1,0:T(8,128)(2,1)S(1)}, u32[]{:S(2)}, u32[]{:S(2)}) collective-permute-start(bf16[16,80,128]{2,1,0:T(8,128)(2,1)S(1)} %get-tuple-element.22), channel_id=1, source_target_pairs={{0,32},{32,0},{1,33},{33,1},{2,34},{34,2},{3,35},{35,3},{4,36},{36... | collective-permute-start | bytes 983048 | tf_op jit(solution)/shard_map/ppermute | solution.py:145
  34.0 33.0 %copy-start.5 = (s32[4]{0:T(128)S(1)}, s32[4]{0:T(128)}, u32[]{:S(2)}) copy-start(s32[4]{0:T(128)} %copy-done.4) | copy-start | bytes 52
  34.0 46.9 %copy-start = (bf16[128,2560]{1,0:T(8,128)(2,1)S(1)}, bf16[128,2560]{1,0:T(8,128)(2,1)}, u32[]{:S(2)}) copy-start(bf16[128,2560]{1,0:T(8,128)(2,1)} %get-tuple-element.30.refs_1_) | copy-start | bytes 1966084
  34.0 23.1 %collective-permute-start.2 = (bf16[128,2560]{1,0:T(8,128)(2,1)}, bf16[128,2560]{1,0:T(8,128)(2,1)S(1)}, u32[]{:S(2)}, u32[]{:S(2)}) collective-permute-start(bf16[128,2560]{1,0:T(8,128)(2,1)} %get-tuple-element.31), channel_id=1, source_target_pairs={{0,512},{256,768},{512,0},{768,256},{1,513},{257,769},{513,1},{769... | collective-permute-start | bytes 1966088 | tf_op jit(solution)/shard_map/ppermute | solution.py:149
  39.6 27.4 %all-to-all-start.1 = ((bf16[16,80,128]{2,1,0:T(8,128)(2,1)}), bf16[16,80,128]{2,1,0:T(8,128)(2,1)S(1)}, u32[]{:S(2)}, u32[]{:S(2)}) async-start(bf16[16,80,128]{2,1,0:T(8,128)(2,1)} %add_convert_fusion), calls=%async_computation.1 | async-start | bytes 655360 | tf_op jit(solution)/shard_map/all_to_all | solution.py:157
  44.9 12.9 %collective-permute-start.4 = (bf16[16,80,128]{2,1,0:T(8,128)(2,1)S(1)}, bf16[16,80,128]{2,1,0:T(8,128)(2,1)S(1)}, u32[]{:S(2)}, u32[]{:S(2)}) collective-permute-start(bf16[16,80,128]{2,1,0:T(8,128)(2,1)S(1)} %all-to-all-done), channel_id=1, source_target_pairs={{0,16},{16,0},{1,17},{17,1},{2,18},{18,2},{3,19},{19,3},{4,20},{20... | collective-permute-start | bytes 983048 | tf_op jit(solution)/shard_map/ppermute | solution.py:153
  50.6 30.3 %collective-permute-start.1 = (bf16[128,2560]{1,0:T(8,128)(2,1)}, bf16[128,2560]{1,0:T(8,128)(2,1)S(1)}, u32[]{:S(2)}, u32[]{:S(2)}) collective-permute-start(bf16[128,2560]{1,0:T(8,128)(2,1)} %get-tuple-element.24), channel_id=1, source_target_pairs={{0,256},{256,512},{512,768},{768,0},{1,257},{257,513},{513,769},{7... | collective-permute-start | bytes 1966088 | tf_op jit(solution)/shard_map/ppermute | solution.py:149
  53.8 27.1 %collective-permute-start.3 = (bf16[128,2560]{1,0:T(8,128)(2,1)}, bf16[128,2560]{1,0:T(8,128)(2,1)}, u32[]{:S(2)}, u32[]{:S(2)}) collective-permute-start(bf16[128,2560]{1,0:T(8,128)(2,1)} %get-tuple-element.32), channel_id=1, source_target_pairs={{0,768},{256,0},{512,256},{768,512},{1,769},{257,1},{513,257},{769... | collective-permute-start | bytes 1966088 | tf_op jit(solution)/shard_map/ppermute | solution.py:149
  57.9 23.1 %collective-permute-start.5 = (bf16[2560,128]{1,0:T(8,128)(2,1)S(1)}, bf16[2560,128]{1,0:T(8,128)(2,1)}, u32[]{:S(2)}, u32[]{:S(2)}) collective-permute-start(bf16[2560,128]{1,0:T(8,128)(2,1)S(1)} %bitcast.8), channel_id=1, source_target_pairs={{0,32},{32,0},{1,33},{33,1},{2,34},{34,2},{3,35},{35,3},{4,36},{36... | collective-permute-start | bytes 1966088 | tf_op jit(solution)/shard_map/ppermute | solution.py:172
  68.4 24.4 %all-to-all-start.2 = ((bf16[16,80,128]{2,1,0:T(8,128)(2,1)}), bf16[16,80,128]{2,1,0:T(8,128)(2,1)S(1)}, u32[]{:S(2)}, u32[]{:S(2)}) async-start(bf16[16,80,128]{2,1,0:T(8,128)(2,1)} %get-tuple-element.28), calls=%async_computation.2 | async-start | bytes 655360 | tf_op jit(solution)/shard_map/all_to_all | solution.py:169
  92.7 6.7 %collective-permute-start.6 = (bf16[16,80,128]{2,1,0:T(8,128)(2,1)S(1)}, bf16[16,80,128]{2,1,0:T(8,128)(2,1)S(1)}, u32[]{:S(2)}, u32[]{:S(2)}) collective-permute-start(bf16[16,80,128]{2,1,0:T(8,128)(2,1)S(1)} %all-to-all-done.2.mine_ref), channel_id=1, source_target_pairs={{0,32},{32,0},{1,33},{33,1},{2,34},{34,2},{3,35},{35,3},{4,36},{36... | collective-permute-start | bytes 983048 | tf_op jit(solution)/shard_map/ppermute | solution.py:185
  96.1 10.2 %all-to-all-start.3 = ((bf16[4,128,256]{2,1,0:T(8,128)(2,1)}), bf16[4,128,256]{2,1,0:T(8,128)(2,1)S(1)}, u32[]{:S(2)}, u32[]{:S(2)}) async-start(bf16[4,128,256]{2,1,0:T(8,128)(2,1)} %shard_map.79), calls=%async_computation.3 | async-start | bytes 524288 | tf_op jit(solution)/shard_map/all_to_all | solution.py:183

commit v4 on v3

--- a/solution.py
+++ b/solution.py
@@ -151,10 +151,10 @@
 
     along_z = after(along_z, hands[1])
     far = lax.ppermute(along_z, "yh", flip)
-    far = after(far, dealt[2])
     pair = (after(keep, along_z).astype(F32) + theirs.astype(F32)).astype(BF)
 
     rows = lax.all_to_all(pair, ("x", "yl"), 0, 0, tiled=True)
+    rows = after(rows, dealt[2])
     new_momentum, spread = call(
         lambda *refs: update_kernel(owners * nc, *refs),
         [jax.ShapeDtypeStruct((chunks, LANES), F32), jax.ShapeDtypeStruct((owners, chunks, LANES), BF)],
@@ -182,7 +182,7 @@
     )
     shares = lax.all_to_all(product, "x", 0, 0, tiled=True)
 
-    others = lax.ppermute(after(spread, product), "c", flip)
+    others = lax.ppermute(spread, "c", flip)
     new_base = call(
         weave_kernel,
         jax.ShapeDtypeStruct((base.shape[0], width), BF),

time: 108 us -> 110 us (1.019)
  starting transfers between devices: 72.9 us -> 82.4 us
  waiting for transfers between devices: 14.2 us -> 4.91 us
    ppermute x1, starting transfers between devices: 9.11 us -> 18 us  [on_device(): swapped = lax.ppermute(quarter, 'c', flip)]
    all_to_all x1, waiting for transfers between devices: 8.63 us -> 0.01 us  [on_device(): spread = lax.all_to_all(spread, ('x', 'yl'), 0, 0, tiled=True)]
    ppermute x1, starting transfers between devices: 3.31 us -> 8.86 us  [on_device(): others = lax.ppermute(spread, 'c', flip)]
    all_to_all x1, starting transfers between devices: 12.5 us -> 7.57 us  [on_device(): spread = lax.all_to_all(spread, ('x', 'yl'), 0, 0, tiled=True)]
    unnamed x12 -> x14, local copies, waits for them, and re-layouts: 2.19 us -> 2.84 us
  transfers between devices with their start and end apart: 11 -> 11, of which waited for: 3 -> 1; matrix products, arithmetic and copies ran while one was open for 1% -> 2% of each run, Pallas kernels for 13% -> 13%
where the time goes in v4:
time: 110 us; the launch traced here: 109 us
  starting transfers between devices  82.4 us (75%)
  Pallas kernels  13.6 us (12%)
  waiting for transfers between devices  4.91 us (4%)
  local copies, waits for them, and re-layouts  4.35 us (4%)
  other arithmetic  2.58 us (2%)
    all_to_all x1, starting transfers between devices, on_device(): along_z = lax.all_to_all(mine, 'z', 0, 0, tiled=True)  19.4 us
    ppermute x1, starting transfers between devices, on_device(): swapped = lax.ppermute(quarter, 'c', flip)  18 us
    ppermute x3, starting transfers between devices, on_device(): lax.ppermute(hands[k], 'x', [(i, (i + k) % nx) for i in range(nx)])  11.2 us
    ppermute x1, starting transfers between devices, on_device(): others = lax.ppermute(spread, 'c', flip)  8.86 us
    pallas_call x4, Pallas kernels, call(): pl.pallas_call(kernel, in_specs=[SMEM] + [pl.BlockSpec(memory_space=pltpu...  8.1 us
    all_to_all x1, starting transfers between devices, on_device(): spread = lax.all_to_all(spread, ('x', 'yl'), 0, 0, tiled=True)  7.57 us
    ppermute x1, starting transfers between devices, on_device(): far = lax.ppermute(along_z, 'yh', flip)  5.7 us
    pallas_call x1, Pallas kernels, deal_tokens(): pl.pallas_call(lambda *refs: deal_kernel(piece, *refs), grid_spec=pltpu.P...  5.54 us
  transfers between devices with their start and end apart: 11, of which 1 were waited for; matrix products, arithmetic and copies ran while one was open for 2% of the time, Pallas kernels for 13%

profile of v4, /device:TPU:1, one launch (start us, length us, event | category | flops | bytes accessed | tf_op | source)
XLA Modules:
  0.0 108.7 jit_solution(13023995615132931419)
XLA Ops:
  0.6 0.7 dynamic_slice.3
  1.4 0.8 broadcast_in_dim.3
  2.1 19.4 %all-to-all-start = ((bf16[16,80,128]{2,1,0:T(8,128)(2,1)}), bf16[16,80,128]{2,1,0:T(8,128)(2,1)S(1)}, u32[]{:S(2)}, u32[]{:S(2)}) async-start(bf16[16,80,128]{2,1,0:T(8,128)(2,1)} %broadcast_in_dim.3), calls=%async_computation | async-start | bytes 655360 | tf_op jit(solution)/shard_map/all_to_all | solution.py:142
  21.6 0.1 pad_add_fusion.where_ref.refs_0_
  21.7 1.1 copy-done.1
  22.8 1.1 copy-done.2
  23.8 1.7 %shard_map.76 = (bf16[16,80,128]{2,1,0:T(8,128)(2,1)S(1)}, bf16[16,80,128]{2,1,0:T(8,128)(2,1)S(1)}, f32[80,128]{1,0:T(8,128)S(1)}) custom-call(s32[4]{0:T(128)S(1)} %pad_add_fusion.where_ref.refs_0_, bf16[32,10240]{1,0:T(8,128)(2,1)S(1)} %bitcast.10, bf16[32,10240]{1,0:T(8,128)(2,1)S(1)} %copy-done.2), custom_call_target="tpu_custom_call" | custom-call | bytes 1000000 | tf_op jit(solution)/shard_map/pallas_call | solution.py:18
  25.6 2.9 %collective-permute-start = (bf16[16,80,128]{2,1,0:T(8,128)(2,1)S(1)}, bf16[16,80,128]{2,1,0:T(8,128)(2,1)S(1)}, u32[]{:S(2)}, u32[]{:S(2)}) collective-permute-start(bf16[16,80,128]{2,1,0:T(8,128)(2,1)S(1)} %get-tuple-element.21), channel_id=1, source_target_pairs={{0,32},{32,0},{1,33},{33,1},{2,34},{34,2},{3,35},{35,3},{4,36},{36... | collective-permute-start | bytes 983048 | tf_op jit(solution)/shard_map/ppermute | solution.py:145
  28.4 5.5 %shard_map.77 = (bf16[128,2560]{1,0:T(8,128)(2,1)}, bf16[128,2560]{1,0:T(8,128)(2,1)}, bf16[128,2560]{1,0:T(8,128)(2,1)}, bf16[128,2560]{1,0:T(8,128)(2,1)}) custom-call(s32[4]{0:T(128)} %copy-done.4, bf16[128,10240]{1,0:T(8,128)(2,1)} %refs_1_), custom_call_target="tpu_custom_call" | custom-call | bytes 1000000 | tf_op jit(solution)/shard_map/pallas_call | solution.py:101
  34.0 4.7 %collective-permute-start.1 = (bf16[128,2560]{1,0:T(8,128)(2,1)}, bf16[128,2560]{1,0:T(8,128)(2,1)S(1)}, u32[]{:S(2)}, u32[]{:S(2)}) collective-permute-start(bf16[128,2560]{1,0:T(8,128)(2,1)} %get-tuple-element.26), channel_id=1, source_target_pairs={{0,512},{256,768},{512,0},{768,256},{1,513},{257,769},{513,1},{769... | collective-permute-start | bytes 1966088 | tf_op jit(solution)/shard_map/ppermute | solution.py:149
  38.7 0.0 all-to-all-done
  38.8 0.8 add_convert_fusion
  39.6 5.3 %all-to-all-start.1 = ((bf16[16,80,128]{2,1,0:T(8,128)(2,1)}), bf16[16,80,128]{2,1,0:T(8,128)(2,1)S(1)}, u32[]{:S(2)}, u32[]{:S(2)}) async-start(bf16[16,80,128]{2,1,0:T(8,128)(2,1)} %add_convert_fusion), calls=%async_computation.1 | async-start | bytes 655360 | tf_op jit(solution)/shard_map/all_to_all | solution.py:156
  44.9 5.7 %collective-permute-start.5 = (bf16[16,80,128]{2,1,0:T(8,128)(2,1)S(1)}, bf16[16,80,128]{2,1,0:T(8,128)(2,1)}, u32[]{:S(2)}, u32[]{:S(2)}) collective-permute-start(bf16[16,80,128]{2,1,0:T(8,128)(2,1)S(1)} %all-to-all-done), channel_id=1, source_target_pairs={{0,16},{16,0},{1,17},{17,1},{2,18},{18,2},{3,19},{19,3},{4,20},{20... | collective-permute-start | bytes 983048 | tf_op jit(solution)/shard_map/ppermute | solution.py:153
  50.6 3.2 %collective-permute-start.3 = (bf16[128,2560]{1,0:T(8,128)(2,1)}, bf16[128,2560]{1,0:T(8,128)(2,1)S(1)}, u32[]{:S(2)}, u32[]{:S(2)}) collective-permute-start(bf16[128,2560]{1,0:T(8,128)(2,1)} %get-tuple-element.23), channel_id=1, source_target_pairs={{0,256},{256,512},{512,768},{768,0},{1,257},{257,513},{513,769},{7... | collective-permute-start | bytes 1966088 | tf_op jit(solution)/shard_map/ppermute | solution.py:149
  53.8 3.3 %collective-permute-start.4 = (bf16[128,2560]{1,0:T(8,128)(2,1)}, bf16[128,2560]{1,0:T(8,128)(2,1)}, u32[]{:S(2)}, u32[]{:S(2)}) collective-permute-start(bf16[128,2560]{1,0:T(8,128)(2,1)} %get-tuple-element.33), channel_id=1, source_target_pairs={{0,768},{256,0},{512,256},{768,512},{1,769},{257,1},{513,257},{769... | collective-permute-start | bytes 1966088 | tf_op jit(solution)/shard_map/ppermute | solution.py:149
  57.1 0.0 collective-permute-done.1.refs_3_
  57.1 0.0 all-to-all-done.1.refs_1_
  57.1 0.0 copy-start.5
  57.1 0.6 copy-done.5
  57.8 1.3 %shard_map.78 = (f32[80,128]{1,0:T(8,128)}, bf16[16,80,128]{2,1,0:T(8,128)(2,1)}) custom-call(s32[4]{0:T(128)S(1)} %copy-done.5, bf16[16,80,128]{2,1,0:T(8,128)(2,1)S(1)} %all-to-all-done.1.refs_1_, f32[80,128]{1,0:T(8,128)S(1)} %bitcast.11, f32[80,128]{1,0:T(8,128)S(1)} %get-tuple-element.28.refs_3_), custom_call_target="tpu_custom_call" | custom-call | bytes 1000000 | tf_op jit(solution)/shard_map/pallas_call | solution.py:18
  59.1 7.6 %all-to-all-start.2 = ((bf16[16,80,128]{2,1,0:T(8,128)(2,1)}), bf16[16,80,128]{2,1,0:T(8,128)(2,1)S(1)}, u32[]{:S(2)}, u32[]{:S(2)}) async-start(bf16[16,80,128]{2,1,0:T(8,128)(2,1)} %get-tuple-element.29), calls=%async_computation.2 | async-start | bytes 655360 | tf_op jit(solution)/shard_map/all_to_all | solution.py:169
  66.7 0.0 collective-permute-done.5
  66.7 1.0 pad_maximum_fusion
  67.7 18.0 %collective-permute-start.6 = (bf16[2560,128]{1,0:T(8,128)(2,1)S(1)}, bf16[2560,128]{1,0:T(8,128)(2,1)}, u32[]{:S(2)}, u32[]{:S(2)}) collective-permute-start(bf16[2560,128]{1,0:T(8,128)(2,1)S(1)} %bitcast.8), channel_id=1, source_target_pairs={{0,32},{32,0},{1,33},{33,1},{2,34},{34,2},{3,35},{35,3},{4,36},{36... | collective-permute-start | bytes 1966088 | tf_op jit(solution)/shard_map/ppermute | solution.py:172
  85.8 0.0 all-to-all-done.2.mine_ref
  85.8 8.9 %collective-permute-start.2 = (bf16[16,80,128]{2,1,0:T(8,128)(2,1)S(1)}, bf16[16,80,128]{2,1,0:T(8,128)(2,1)S(1)}, u32[]{:S(2)}, u32[]{:S(2)}) collective-permute-start(bf16[16,80,128]{2,1,0:T(8,128)(2,1)S(1)} %all-to-all-done.2.mine_ref), channel_id=1, source_target_pairs={{0,32},{32,0},{1,33},{33,1},{2,34},{34,2},{3,35},{35,3},{4,36},{36... | collective-permute-start | bytes 983048 | tf_op jit(solution)/shard_map/ppermute | solution.py:185
  94.7 3.2 %shard_map.80 = bf16[4,128,256]{2,1,0:T(8,128)(2,1)} custom-call(s32[4]{0:T(128)S(1)} %copy-done.6, bf16[128,2560]{1,0:T(8,128)(2,1)S(1)} %copy-done, bf16[128,2560]{1,0:T(8,128)(2,1)S(1)} %collective-permute-done.3.refs_2_, bf16[128,2560]{1,0:T(8,128)(2,1)S(1)} %collective-permute-done.1.refs_3_, bf16[128,2560]{1,0:T(8,128)(2,1)} %collective-permute-done.4.refs_4_, ...), custom_call_target="tpu_custom_call" | custom-call | bytes 1000000 | tf_op jit(solution)/shard_map/pallas_call | solution.py:18
  97.9 3.4 %all-to-all-start.3 = ((bf16[4,128,256]{2,1,0:T(8,128)(2,1)}), bf16[4,128,256]{2,1,0:T(8,128)(2,1)S(1)}, u32[]{:S(2)}, u32[]{:S(2)}) async-start(bf16[4,128,256]{2,1,0:T(8,128)(2,1)} %shard_map.80), calls=%async_computation.3 | async-start | bytes 524288 | tf_op jit(solution)/shard_map/all_to_all | solution.py:183
  101.3 1.9 %shard_map.79 = bf16[32,10240]{1,0:T(8,128)(2,1)} custom-call(s32[4]{0:T(128)S(1)} %copy-done.6, bf16[16,80,128]{2,1,0:T(8,128)(2,1)S(1)} %all-to-all-done.2.mine_ref, bf16[16,80,128]{2,1,0:T(8,128)(2,1)S(1)} %collective-permute-done.2.other_ref), custom_call_target="tpu_custom_call" | custom-call | bytes 1000000 | tf_op jit(solution)/shard_map/pallas_call | solution.py:18
  103.2 4.9 %all-to-all-done.3 = bf16[4,128,256]{2,1,0:T(8,128)(2,1)S(1)} async-done(((bf16[4,128,256]{2,1,0:T(8,128)(2,1)}), bf16[4,128,256]{2,1,0:T(8,128)(2,1)S(1)}, u32[]{:S(2)}, u32[]{:S(2)}) %all-to-all-start.3) | async-done | bytes 262176 | tf_op jit(solution)/shard_map/all_to_all | solution.py:183
  108.1 0.7 reduce_sum.12
  (15 shorter events, 0.0 us)
Async XLA Ops:
  2.1 36.6 %all-to-all-start = ((bf16[16,80,128]{2,1,0:T(8,128)(2,1)}), bf16[16,80,128]{2,1,0:T(8,128)(2,1)S(1)}, u32[]{:S(2)}, u32[]{:S(2)}) async-start(bf16[16,80,128]{2,1,0:T(8,128)(2,1)} %broadcast_in_dim.3), calls=%async_computation | async-start | bytes 655360 | tf_op jit(solution)/shard_map/all_to_all | solution.py:142
  21.7 1.1 %copy-start.1 = (bf16[1,32,10240]{2,1,0:T(8,128)(2,1)S(1)}, bf16[1,32,10240]{2,1,0:T(8,128)(2,1)}, u32[]{:S(2)}) copy-start(bf16[1,32,10240]{2,1,0:T(8,128)(2,1)} %param.5) | copy-start | bytes 1966084
  22.8 1.1 copy-start.2
  23.8 4.6 %copy-start.4 = (s32[4]{0:T(128)}, s32[4]{0:T(128)S(1)}, u32[]{:S(2)}) copy-start(s32[4]{0:T(128)S(1)} %pad_add_fusion.where_ref.refs_0_) | copy-start | bytes 52
  23.8 33.3 %copy-start.3 = (f32[1,10240]{1,0:T(1,128)S(1)}, f32[1,10240]{1,0:T(1,128)}, u32[]{:S(2)}) copy-start(f32[1,10240]{1,0:T(1,128)} %param.7) | copy-start | bytes 122884
  25.6 13.2 %collective-permute-start = (bf16[16,80,128]{2,1,0:T(8,128)(2,1)S(1)}, bf16[16,80,128]{2,1,0:T(8,128)(2,1)S(1)}, u32[]{:S(2)}, u32[]{:S(2)}) collective-permute-start(bf16[16,80,128]{2,1,0:T(8,128)(2,1)S(1)} %get-tuple-element.21), channel_id=1, source_target_pairs={{0,32},{32,0},{1,33},{33,1},{2,34},{34,2},{3,35},{35,3},{4,36},{36... | collective-permute-start | bytes 983048 | tf_op jit(solution)/shard_map/ppermute | solution.py:145
  34.0 60.7 %copy-start = (bf16[128,2560]{1,0:T(8,128)(2,1)S(1)}, bf16[128,2560]{1,0:T(8,128)(2,1)}, u32[]{:S(2)}) copy-start(bf16[128,2560]{1,0:T(8,128)(2,1)} %get-tuple-element.32.refs_1_) | copy-start | bytes 1966084
  34.0 60.7 %copy-start.6 = (s32[4]{0:T(128)S(1)}, s32[4]{0:T(128)}, u32[]{:S(2)}) copy-start(s32[4]{0:T(128)} %copy-done.4) | copy-start | bytes 52
  34.0 23.1 %collective-permute-start.1 = (bf16[128,2560]{1,0:T(8,128)(2,1)}, bf16[128,2560]{1,0:T(8,128)(2,1)S(1)}, u32[]{:S(2)}, u32[]{:S(2)}) collective-permute-start(bf16[128,2560]{1,0:T(8,128)(2,1)} %get-tuple-element.26), channel_id=1, source_target_pairs={{0,512},{256,768},{512,0},{768,256},{1,513},{257,769},{513,1},{769... | collective-permute-start | bytes 1966088 | tf_op jit(solution)/shard_map/ppermute | solution.py:149
  39.6 17.5 %all-to-all-start.1 = ((bf16[16,80,128]{2,1,0:T(8,128)(2,1)}), bf16[16,80,128]{2,1,0:T(8,128)(2,1)S(1)}, u32[]{:S(2)}, u32[]{:S(2)}) async-start(bf16[16,80,128]{2,1,0:T(8,128)(2,1)} %add_convert_fusion), calls=%async_computation.1 | async-start | bytes 655360 | tf_op jit(solution)/shard_map/all_to_all | solution.py:156
  44.9 21.8 %collective-permute-start.5 = (bf16[16,80,128]{2,1,0:T(8,128)(2,1)S(1)}, bf16[16,80,128]{2,1,0:T(8,128)(2,1)}, u32[]{:S(2)}, u32[]{:S(2)}) collective-permute-start(bf16[16,80,128]{2,1,0:T(8,128)(2,1)S(1)} %all-to-all-done), channel_id=1, source_target_pairs={{0,16},{16,0},{1,17},{17,1},{2,18},{18,2},{3,19},{19,3},{4,20},{20... | collective-permute-start | bytes 983048 | tf_op jit(solution)/shard_map/ppermute | solution.py:153
  50.6 44.1 %collective-permute-start.3 = (bf16[128,2560]{1,0:T(8,128)(2,1)}, bf16[128,2560]{1,0:T(8,128)(2,1)S(1)}, u32[]{:S(2)}, u32[]{:S(2)}) collective-permute-start(bf16[128,2560]{1,0:T(8,128)(2,1)} %get-tuple-element.23), channel_id=1, source_target_pairs={{0,256},{256,512},{512,768},{768,0},{1,257},{257,513},{513,769},{7... | collective-permute-start | bytes 1966088 | tf_op jit(solution)/shard_map/ppermute | solution.py:149
  53.8 40.9 %collective-permute-start.4 = (bf16[128,2560]{1,0:T(8,128)(2,1)}, bf16[128,2560]{1,0:T(8,128)(2,1)}, u32[]{:S(2)}, u32[]{:S(2)}) collective-permute-start(bf16[128,2560]{1,0:T(8,128)(2,1)} %get-tuple-element.33), channel_id=1, source_target_pairs={{0,768},{256,0},{512,256},{768,512},{1,769},{257,1},{513,257},{769... | collective-permute-start | bytes 1966088 | tf_op jit(solution)/shard_map/ppermute | solution.py:149
  57.1 0.7 copy-start.5
  59.1 26.7 %all-to-all-start.2 = ((bf16[16,80,128]{2,1,0:T(8,128)(2,1)}), bf16[16,80,128]{2,1,0:T(8,128)(2,1)S(1)}, u32[]{:S(2)}, u32[]{:S(2)}) async-start(bf16[16,80,128]{2,1,0:T(8,128)(2,1)} %get-tuple-element.29), calls=%async_computation.2 | async-start | bytes 655360 | tf_op jit(solution)/shard_map/all_to_all | solution.py:169
  67.7 26.9 %collective-permute-start.6 = (bf16[2560,128]{1,0:T(8,128)(2,1)S(1)}, bf16[2560,128]{1,0:T(8,128)(2,1)}, u32[]{:S(2)}, u32[]{:S(2)}) collective-permute-start(bf16[2560,128]{1,0:T(8,128)(2,1)S(1)} %bitcast.8), channel_id=1, source_target_pairs={{0,32},{32,0},{1,33},{33,1},{2,34},{34,2},{3,35},{35,3},{4,36},{36... | collective-permute-start | bytes 1966088 | tf_op jit(solution)/shard_map/ppermute | solution.py:172
  85.8 15.5 %collective-permute-start.2 = (bf16[16,80,128]{2,1,0:T(8,128)(2,1)S(1)}, bf16[16,80,128]{2,1,0:T(8,128)(2,1)S(1)}, u32[]{:S(2)}, u32[]{:S(2)}) collective-permute-start(bf16[16,80,128]{2,1,0:T(8,128)(2,1)S(1)} %all-to-all-done.2.mine_ref), channel_id=1, source_target_pairs={{0,32},{32,0},{1,33},{33,1},{2,34},{34,2},{3,35},{35,3},{4,36},{36... | collective-permute-start | bytes 983048 | tf_op jit(solution)/shard_map/ppermute | solution.py:185
  97.9 10.2 %all-to-all-start.3 = ((bf16[4,128,256]{2,1,0:T(8,128)(2,1)}), bf16[4,128,256]{2,1,0:T(8,128)(2,1)S(1)}, u32[]{:S(2)}, u32[]{:S(2)}) async-start(bf16[4,128,256]{2,1,0:T(8,128)(2,1)} %shard_map.80), calls=%async_computation.3 | async-start | bytes 524288 | tf_op jit(solution)/shard_map/all_to_all | solution.py:183
